TPU v7x, 256 devices: a whole 4x4x8 slice. The times are simulated.
256 devices in a mesh: group: 8 (over x_hi, y), blk: 32 (over x_lo, z, core).
Axes of the slice: x: 4 (x_hi: 2, x_lo: 2; x = x_hi * 2 + x_lo), y: 4, z: 8, core: 2. Of those that a mesh axis runs over, the one named last changes fastest.
Arguments:
- queries: bfloat16 [256, 24, 128], P(('group', 'blk')), may hold values from -0.59765625 to 0.59765625
- query_len: int32 [256], replicated, may hold values from 1 to 24
- pages: bfloat16 [1536, 1030, 128], P(('group', 'blk')), may hold values from -6 to 6
- page_count: int32 [768], P(('group', 'blk')), may hold values from 1 to 2, as said below
- page_offset: int32 [768], P(('group', 'blk')), may hold values from 0 to 4, as said below
- helper_doc: int32 [1536], P(('group', 'blk')), may hold values from -1 to 11, as said below
Outputs:
- scores: float32 [768, 256], P(('group', 'blk'))
Inputs may be any that keep to these rules, and one draw needn't show every extreme that they name: `page_count`: every document has at least one home page; a device's home ranges do not intersect and lie back to back from slot 0, in an order of its own documents. `page_offset`: offsets are within the owner's slots and are consistent with page_count as stated there. helper_doc is -1 exactly on home slots; elsewhere it is s * 3 + j with 1 <= s <= 3. Home slots come before helper slots on each device.
All inputs are finite; a program needn't handle non-finite values.
Results may differ from a plain program's by a relative error of at most 0.0003.
Values may be sent and summed in bfloat16 or wider, within the bound.
No kernel may reach another device: no remote copies, remote signals or barrier semaphores. Data moves between devices by JAX's collectives and lax.ppermute only.
A program may use at most 64 MiB of HBM per device.

v0:
```python
import jax
import jax.numpy as jnp
from jax import lax
from jax.sharding import PartitionSpec as P

SPILL = 3


lowest = -1e30


def shifted(value, axis, steps):
    count = lax.axis_size(axis)
    pairs = [(source, (source + steps) % count) for source in range(count)]
    return lax.ppermute(value, axis, pairs)


def slot_table(page_count, page_offset, helper_doc, slot_total):
    positions = jnp.arange(helper_doc.shape[0], dtype=jnp.int32)[None, :]
    inside = (positions >= page_offset[:, None]) & (
        positions < page_offset[:, None] + page_count[:, None]
    )
    home_doc = jnp.sum(
        jnp.where(inside, jnp.arange(page_count.shape[0], dtype=jnp.int32)[:, None], 0), axis=0
    )
    slots = jnp.where(jnp.any(inside, axis=0), home_doc, helper_doc)
    return slots[None, :] == jnp.arange(slot_total, dtype=jnp.int32)[:, None]


def page_maxima(pages, member, query_block, slot_total):
    token_rows = query_block.reshape(-1, query_block.shape[2])

    def visit(page_index, running):
        page_rows = lax.dynamic_index_in_dim(pages, page_index, 0, keepdims=False)
        scores = lax.dot_general(
            page_rows, token_rows, (((1,), (1,)), ((), ())), preferred_element_type=jnp.float32
        )
        patch_best = jnp.max(scores, axis=0)
        chosen = lax.dynamic_index_in_dim(member, page_index, 1, keepdims=True)
        return jnp.where(chosen, jnp.maximum(running, patch_best[None, :]), running)

    start_value = jnp.full((slot_total, token_rows.shape[0]), lowest, jnp.float32)
    return lax.fori_loop(0, pages.shape[0], visit, start_value)


def local(queries, query_len, pages, page_count, page_offset, helper_doc):
    doc_local = page_count.shape[0]
    tokens_per = queries.shape[1]
    slot_total = (SPILL + 1) * doc_local
    member = slot_table(page_count, page_offset, helper_doc, slot_total)
    query_total = query_len.shape[0]
    block_max = page_maxima(
        pages, member, lax.all_gather(queries, ("group", "blk"), axis=0, tiled=True), slot_total
    )
    partial_value = block_max
    partial_value = partial_value.reshape(SPILL + 1, doc_local, query_total * tokens_per)
    doc_best = partial_value[0]
    for distance in range(1, SPILL + 1):
        doc_best = jnp.maximum(doc_best, shifted(partial_value[distance], "blk", -distance))
    doc_best = doc_best.reshape(doc_local, query_total, tokens_per)
    valid = jnp.arange(tokens_per, dtype=jnp.int32)[None, :] < query_len[:, None]
    totals = jnp.sum(jnp.where(valid[None], doc_best, jnp.float32(0.0)), axis=2)
    return totals / query_len.astype(jnp.float32)[None, :]


def solution(mesh):
    return jax.shard_map(
        local,
        mesh=mesh,
        in_specs=(
            P(("group", "blk"), None, None),
            P(),
            P(("group", "blk"), None, None),
            P(("group", "blk")),
            P(("group", "blk")),
            P(("group", "blk")),
        ),
        out_specs=P(("group", "blk"), None),
        check_vma=False,
    )
```

profile of v0, /device:TPU:1, one launch (start us, length us, event | category | flops | bytes accessed | tf_op | source)
XLA Modules:
  0.0 467.7 jit_solution(6319344564781232513)
XLA Ops:
  6.5 0.7 all-gather.2.cloned.1.call-update
  7.3 0.7 add.28
  7.9 0.7 fusion.4
  8.7 0.7 select_reduce_fusion.1
  9.4 0.7 select_n.29
  10.2 406.4 %all-gather.2.cloned.1.call-done = bf16[256,24,128]{2,1,0:T(8,128)(2,1)} async-done(((bf16[1,24,128]{2,1,0:T(8,128)(2,1)}), bf16[256,24,128]{2,1,0:T(8,128)(2,1)}) %all-gather.2.cloned.1.call-update) | async-done | bytes 1572880 | tf_op jit(solution)/shard_map/all_gather | solution.py:53
  416.6 31.0 %while.14 = (s32[]{:T(128)}, f32[12,6144]{1,0:T(8,128)S(1)}, pred[12,6]{0,1:T(8,128)(4,1)S(1)}, bf16[6,1030,128]{2,1,0:T(8,128)(2,1)}, bf16[6144,128]{1,0:T(8,128)(2,1)}, /*index=5*/s32[]{:T(128)}, s32[]{:T(128)}) while((s32[]{:T(128)}, f32[12,6144]{1,0:T(8,128)S(1)}, pred[12,6]{0,1:T(8,128)(4,1)S(1)}, ...), condition=%wide.region_4.5_spmd.clone, body=%wide.region_2.4_spmd.clone.sunk | while | flops 1626593280 | bytes 2476671 | solution.py:43
  416.6 5.0 %convolution_reduce_fusion.2 = f32[6144]{0:T(1024)S(1)} fusion(bf16[6144,128]{1,0:T(8,128)(2,1)} %get-tuple-element.180, bf16[6,1030,128]{2,1,0:T(8,128)(2,1)} %get-tuple-element.179, s32[]{:T(128)} %get-tuple-element.169), kind=kOutput, calls=%fused_computation.clone.1 | convolution fusion | flops 1626372096 | bytes 1862144 | tf_op jit(solution)/shard_map/while/body/eval_jaxpr/dot_general | solution.py:35
  421.6 0.1 maximum_select_fusion.2
  421.7 5.0 %convolution_reduce_fusion.2 = f32[6144]{0:T(1024)S(1)} fusion(bf16[6144,128]{1,0:T(8,128)(2,1)} %get-tuple-element.180, bf16[6,1030,128]{2,1,0:T(8,128)(2,1)} %get-tuple-element.179, s32[]{:T(128)} %get-tuple-element.169), kind=kOutput, calls=%fused_computation.clone.1 | convolution fusion | flops 1626372096 | bytes 1862144 | tf_op jit(solution)/shard_map/while/body/eval_jaxpr/dot_general | solution.py:35
  426.8 0.1 maximum_select_fusion.2
  426.9 5.0 %convolution_reduce_fusion.2 = f32[6144]{0:T(1024)S(1)} fusion(bf16[6144,128]{1,0:T(8,128)(2,1)} %get-tuple-element.180, bf16[6,1030,128]{2,1,0:T(8,128)(2,1)} %get-tuple-element.179, s32[]{:T(128)} %get-tuple-element.169), kind=kOutput, calls=%fused_computation.clone.1 | convolution fusion | flops 1626372096 | bytes 1862144 | tf_op jit(solution)/shard_map/while/body/eval_jaxpr/dot_general | solution.py:35
  431.9 0.1 maximum_select_fusion.2
  432.1 5.0 %convolution_reduce_fusion.2 = f32[6144]{0:T(1024)S(1)} fusion(bf16[6144,128]{1,0:T(8,128)(2,1)} %get-tuple-element.180, bf16[6,1030,128]{2,1,0:T(8,128)(2,1)} %get-tuple-element.179, s32[]{:T(128)} %get-tuple-element.169), kind=kOutput, calls=%fused_computation.clone.1 | convolution fusion | flops 1626372096 | bytes 1862144 | tf_op jit(solution)/shard_map/while/body/eval_jaxpr/dot_general | solution.py:35
  437.2 5.0 %convolution_reduce_fusion.2 = f32[6144]{0:T(1024)S(1)} fusion(bf16[6144,128]{1,0:T(8,128)(2,1)} %get-tuple-element.180, bf16[6,1030,128]{2,1,0:T(8,128)(2,1)} %get-tuple-element.179, s32[]{:T(128)} %get-tuple-element.169), kind=kOutput, calls=%fused_computation.clone.1 | convolution fusion | flops 1626372096 | bytes 1862144 | tf_op jit(solution)/shard_map/while/body/eval_jaxpr/dot_general | solution.py:35
  442.4 5.0 %convolution_reduce_fusion.2 = f32[6144]{0:T(1024)S(1)} fusion(bf16[6144,128]{1,0:T(8,128)(2,1)} %get-tuple-element.180, bf16[6,1030,128]{2,1,0:T(8,128)(2,1)} %get-tuple-element.179, s32[]{:T(128)} %get-tuple-element.169), kind=kOutput, calls=%fused_computation.clone.1 | convolution fusion | flops 1626372096 | bytes 1862144 | tf_op jit(solution)/shard_map/while/body/eval_jaxpr/dot_general | solution.py:35
  447.6 3.2 collective-permute-start
  450.8 1.2 collective-permute-start.1
  452.2 1.5 collective-permute-done
  453.6 1.8 collective-permute-done.1
  455.5 4.2 collective-permute-done.2
  459.7 0.3 reshape.40
  460.0 0.2 select_reduce_fusion
  460.2 0.6 broadcast_divide_fusion
  (19 shorter events, 0.7 us)
Async XLA Ops:
  6.5 410.0 %all-gather.2.cloned.1.call-start = ((), (), s32[]{:S(2)}) async-start(), calls=%async_computation | async-start | bytes 1579008 | tf_op jit(solution)/shard_map/all_gather | solution.py:53
  416.6 35.5 %copy-start = (s32[256]{0:T(256)S(1)}, s32[256]{0:T(256)}, u32[]{:S(2)}) copy-start(s32[256]{0:T(256)} %param.9) | copy-start | bytes 3076
  447.6 6.0 %collective-permute-start = (f32[3,6144]{1,0:T(4,128)S(1)}, f32[3,6144]{1,0:T(4,128)S(1)}, u32[]{:S(2)}, u32[]{:S(2)}) collective-permute-start(f32[3,6144]{1,0:T(4,128)S(1)} %get-tuple-element.128), channel_id=1, source_target_pairs={{0,31},{1,0},{2,1},{3,2},{4,3},{5,4},{6,5},{7,6},{8,7},{9,8},{10,9... | collective-permute-start | bytes 221192 | tf_op jit(solution)/shard_map/ppermute | solution.py:15
  450.8 4.7 %collective-permute-start.1 = (f32[3,6144]{1,0:T(4,128)S(1)}, f32[3,6144]{1,0:T(4,128)S(1)}, u32[]{:S(2)}, u32[]{:S(2)}) collective-permute-start(f32[3,6144]{1,0:T(4,128)S(1)} %get-tuple-element.130), channel_id=1, source_target_pairs={{0,30},{1,31},{2,0},{3,1},{4,2},{5,3},{6,4},{7,5},{8,6},{9,7},{10,... | collective-permute-start | bytes 221192 | tf_op jit(solution)/shard_map/ppermute | solution.py:15
  452.0 7.7 %collective-permute-start.2 = (f32[3,6144]{1,0:T(4,128)S(1)}, f32[3,6144]{1,0:T(4,128)S(1)}, u32[]{:S(2)}, u32[]{:S(2)}) collective-permute-start(f32[3,6144]{1,0:T(4,128)S(1)} %get-tuple-element.129), channel_id=1, source_target_pairs={{0,29},{1,30},{2,31},{3,0},{4,1},{5,2},{6,3},{7,4},{8,5},{9,6},{10... | collective-permute-start | bytes 221192 | tf_op jit(solution)/shard_map/ppermute | solution.py:15
Sparse Core Ops, SparseCore 0:
  9.2 407.2 all-gather.1
where the time goes:
time: 468 us
  waiting for transfers between devices  415 us (89%)
  matrix products  30.1 us (6%)
  between operations  13.4 us (3%)
    all_gather x1, waiting for transfers between devices, local(): lax.all_gather(queries, ('group', 'blk'), axis=0, tiled=True)  406 us
    dot_general x6, matrix products, visit(): lax.dot_general(page_rows, token_rows, (((1,), (1,)), ((), ())), preferre...  30.1 us
  transfers between devices with their start and end apart: 4, of which 4 were waited for; matrix products, arithmetic and copies ran while one was open for 1% of the time, Pallas kernels for 0%

commit v1 on v0

v1 whole, which is shorter than its diff:
```python
import jax
import jax.numpy as jnp
from jax import lax
from jax.experimental import pallas as pl
from jax.experimental.pallas import tpu as pltpu
from jax.sharding import Mesh, PartitionSpec as P

SPILL = 3
SIZES = (2, 4, 2, 8, 2)
AXES = ("xh", "y", "xl", "z", "c")
NX, NY, NZ, NC = 4, 4, 8, 2
CHUNK = NY * NZ
TILE = 512
lowest = -1e30
VMEM_LIMIT = 48 * 1024 * 1024
TRANSPOSED = (((1,), (1,)), ((), ()))


def device_id(x, y, z, c):
    return (((x // 2) * NY + y) * 2 + x % 2) * NZ * NC + z * NC + c


def coordinates():
    return [
        (x, y, z, c) for x in range(NX) for y in range(NY) for z in range(NZ) for c in range(NC)
    ]


def along_x(value, steps):
    pairs = [
        (device_id(x, y, z, c), device_id((x + steps) % NX, y, z, c)) for x, y, z, c in coordinates()
    ]
    return lax.ppermute(value, AXES, pairs)


def other_core(value):
    pairs = [(device_id(x, y, z, c), device_id(x, y, z, 1 - c)) for x, y, z, c in coordinates()]
    return lax.ppermute(value, AXES, pairs)


def along_blk(value, steps):
    count = 32
    pairs = [
        (g * count + b, g * count + (b + steps) % count) for g in range(8) for b in range(count)
    ]
    return lax.ppermute(value, AXES, pairs)


def query_index(x, c, k):
    return device_id(x, k // NZ, k % NZ, c)


def slot_ids(count_ref, offset_ref, helper_ref, pages):
    ids = []
    for k in range(pages):
        slot = helper_ref[k]
        for j in range(count_ref.shape[0]):
            inside = (offset_ref[j] <= k) & (k < offset_ref[j] + count_ref[j])
            slot = jnp.where(inside, j, slot)
        ids.append(jnp.clip(slot, 0, (SPILL + 1) * count_ref.shape[0] - 1))
    return ids


def maxima_kernel(len_ref, count_ref, offset_ref, helper_ref, *rest):
    chunks = rest[: NX * NC]
    pages_ref = rest[NX * NC]
    outs = rest[NX * NC + 1 : NX * NC + 2 + SPILL]
    live_ref, tail_ref, slot_ref = rest[NX * NC + 2 + SPILL :]
    pages, patches, width = pages_ref.shape
    docs = count_ref.shape[0]
    whole = patches // 16 * 16
    rest_rows = patches - whole
    tokens = chunks[0].shape[1]

    for p in range(pages):
        tail_ref[8 * p : 8 * p + rest_rows, :] = pages_ref[p, whole:, :].astype(jnp.float32)
        for extra in range(rest_rows, 8):
            tail_ref[8 * p + extra : 8 * p + extra + 1, :] = pages_ref[
                p, patches - 1 : patches, :
            ].astype(jnp.float32)
    tails = tail_ref[...].astype(jnp.bfloat16)

    x = lax.axis_index("xh") * 2 + lax.axis_index("xl")
    c = lax.axis_index("c")
    totals = []
    for chunk in range(NX * NC):

        def add(k, total, chunk=chunk):
            return total + len_ref[query_index(chunk // NC, chunk % NC, k)]

        totals.append(lax.fori_loop(0, CHUNK, add, jnp.int32(0), unroll=8))
    total = sum(totals)

    for place, steps in enumerate((0, 1, 3, 2)):
        for core in range(NC):
            source = chunks[place * NC + core]
            chunk_x = lax.rem(x + NX - steps, NX)
            chunk_c = c if core == 0 else 1 - c
            chunk_id = chunk_x * NC + chunk_c
            start = jnp.int32(0)
            for other in range(NX * NC):
                start = start + jnp.where(other < chunk_id, totals[other], 0)

            end = start
            for other in range(NX * NC):
                end = end + jnp.where(other == chunk_id, totals[other], 0)
            after = live_ref[pl.ds(end, tokens), :]

            def put(k, at, source=source, chunk_x=chunk_x, chunk_c=chunk_c):
                live_ref[pl.ds(at, tokens), :] = source[k].astype(jnp.float32)
                return at + len_ref[query_index(chunk_x, chunk_c, k)]

            lax.fori_loop(0, CHUNK, put, start, unroll=8)
            live_ref[pl.ds(end, tokens), :] = after
    live_ref[pl.ds(total, TILE), :] = jnp.zeros((TILE, width), jnp.float32)

    ids = slot_ids(count_ref, offset_ref, helper_ref, pages)

    def visit(tile, _):
        at = pl.multiple_of(tile * TILE, TILE)
        token_rows = live_ref[pl.ds(at, TILE), :].astype(jnp.bfloat16)
        tail_scores = lax.dot_general(
            tails, token_rows, TRANSPOSED, preferred_element_type=jnp.float32
        )
        slot_ref[...] = jnp.full(slot_ref.shape, lowest, jnp.float32)
        for p in range(pages):
            scores = lax.dot_general(
                pages_ref[p, :whole, :], token_rows, TRANSPOSED, preferred_element_type=jnp.float32
            )
            best = jnp.max(scores.reshape(whole // 8, 8, TILE), axis=0)
            best = jnp.maximum(best, tail_scores[8 * p : 8 * p + 8])
            best = jnp.max(best, axis=0, keepdims=True)
            slot_ref[ids[p]] = jnp.maximum(slot_ref[ids[p]], best)
        for distance in range(SPILL + 1):
            for j in range(docs):
                outs[distance][j, :, pl.ds(at, TILE)] = slot_ref[distance * docs + j]
        return 0

    lax.fori_loop(0, (total + TILE - 1) // TILE, visit, 0)


def scores_kernel(len_ref, own_ref, one_ref, two_ref, three_ref, out_ref, acc_ref):
    queries = len_ref.shape[1]
    docs = own_ref.shape[0]
    lens = len_ref[...]

    def place(n):
        core = n % NC
        z = (n // NC) % NZ
        x_lo = (n // (NC * NZ)) % 2
        y = (n // (NC * NZ * 2)) % NY
        x_hi = n // (NC * NZ * 2 * NY)
        return (((x_hi * 2 + x_lo) * NC + core) * NY + y) * NZ + z

    before = place(lax.broadcasted_iota(jnp.int32, (queries, queries), 0)) < place(
        lax.broadcasted_iota(jnp.int32, (queries, queries), 1)
    )
    row = jnp.broadcast_to(lens.astype(jnp.float32).astype(jnp.bfloat16), (8, queries))
    starts = jnp.dot(
        row,
        jnp.where(before, 1.0, 0.0).astype(jnp.bfloat16),
        preferred_element_type=jnp.float32,
    )[0:1].astype(jnp.int32)
    ends = starts + lens
    total = jnp.max(ends)
    acc_ref[...] = jnp.zeros(acc_ref.shape, jnp.float32)

    def visit(tile, _):
        at = pl.multiple_of(tile * TILE, TILE)
        columns = lax.broadcasted_iota(jnp.int32, (1, TILE), 1) + at
        parts = []
        for j in range(docs):
            value = jnp.maximum(
                jnp.maximum(own_ref[j, :, pl.ds(at, TILE)], one_ref[j, :, pl.ds(at, TILE)]),
                jnp.maximum(two_ref[j, :, pl.ds(at, TILE)], three_ref[j, :, pl.ds(at, TILE)]),
            )
            value = jnp.where(columns < total, value, 0.0)
            high = value.astype(jnp.bfloat16)
            left = value - high.astype(jnp.float32)
            middle = left.astype(jnp.bfloat16)
            low = (left - middle.astype(jnp.float32)).astype(jnp.bfloat16)
            parts += [high.astype(jnp.float32), middle.astype(jnp.float32), low.astype(jnp.float32)]
        parts.append(jnp.zeros((acc_ref.shape[0] - len(parts), TILE), jnp.float32))
        left_side = jnp.concatenate(parts, axis=0).astype(jnp.bfloat16)
        token = lax.broadcasted_iota(jnp.int32, (TILE, queries), 0) + at
        chosen = jnp.where((token >= starts) & (token < ends), 1.0, 0.0).astype(jnp.bfloat16)
        acc_ref[...] += jnp.dot(left_side, chosen, preferred_element_type=jnp.float32)
        return 0

    lax.fori_loop(0, (total + TILE - 1) // TILE, visit, 0)
    divisor = lens.astype(jnp.float32)
    for j in range(docs):
        summed = (acc_ref[3 * j : 3 * j + 1, :] + acc_ref[3 * j + 1 : 3 * j + 2, :]) + acc_ref[
            3 * j + 2 : 3 * j + 3, :
        ]
        out_ref[j : j + 1, :] = summed / divisor


SMEM = pl.BlockSpec(memory_space=pltpu.SMEM)
VMEM = pl.BlockSpec(memory_space=pltpu.VMEM)


def local(queries, query_len, pages, page_count, page_offset, helper_doc):
    docs = page_count.shape[0]
    total = query_len.shape[0]
    tokens, width = queries.shape[1:]
    columns = total * tokens

    copies = jnp.broadcast_to(queries, (CHUNK, tokens, width))
    mine = lax.all_to_all(copies, ("y", "z"), 0, 0, tiled=True)
    chunks = []
    for steps in (0, 1, 3, 2):
        value = mine if steps == 0 else along_x(mine, steps)
        chunks += [value, other_core(value)]

    maxima = pl.pallas_call(
        maxima_kernel,
        out_shape=[jax.ShapeDtypeStruct((docs, 1, columns), jnp.float32)] * (SPILL + 1),
        in_specs=[SMEM] * 4 + [VMEM] * (len(chunks) + 1),
        out_specs=[VMEM] * (SPILL + 1),
        scratch_shapes=[
            pltpu.VMEM((columns + TILE, width), jnp.float32),
            pltpu.VMEM((8 * pages.shape[0], width), jnp.float32),
            pltpu.VMEM(((SPILL + 1) * docs, 1, TILE), jnp.float32),
        ],
        compiler_params=pltpu.CompilerParams(vmem_limit_bytes=VMEM_LIMIT),
    )(query_len, page_count, page_offset, helper_doc, *chunks, pages)

    arrived = [along_blk(maxima[distance], -distance) for distance in range(1, SPILL + 1)]
    return pl.pallas_call(
        scores_kernel,
        out_shape=jax.ShapeDtypeStruct((docs, total), jnp.float32),
        in_specs=[VMEM] * (SPILL + 2),
        out_specs=VMEM,
        scratch_shapes=[pltpu.VMEM((16, total), jnp.float32)],
        compiler_params=pltpu.CompilerParams(vmem_limit_bytes=VMEM_LIMIT),
    )(query_len[None, :], maxima[0], *arrived)


def solution(mesh):
    split = Mesh(mesh.devices.reshape(SIZES), AXES)
    return jax.shard_map(
        local,
        mesh=split,
        in_specs=(P(AXES, None, None), P(), P(AXES, None, None), P(AXES), P(AXES), P(AXES)),
        out_specs=P(AXES, None),
        check_vma=False,
    )
```

time: 468 us -> 71.1 us (0.15)
  waiting for transfers between devices: 415 us -> 7.11 us
  matrix products: 30.1 us -> 0 us
  blocking collectives: 0 us -> 21.2 us
  Pallas kernels: 0 us -> 20.7 us
  between operations: 13.4 us -> 0.03 us
  starting transfers between devices: 4.44 us -> 17 us
    all_gather x1 -> x0, waiting for transfers between devices: 406 us -> none  [local(): lax.all_gather(queries, ('group', 'blk'), axis=0, tiled=True)]
    dot_general x6 -> x0, matrix products: 30.1 us -> none  [visit(): lax.dot_general(page_rows, token_rows, (((1,), (1,)), ((), ())), preferre...]
    all_to_all x0 -> x1, blocking collectives: none -> 21.2 us  [local(): mine = lax.all_to_all(copies, ('y', 'z'), 0, 0, tiled=True)]
    pallas_call x0 -> x2, Pallas kernels: none -> 20.7 us  [the longest x1 18.1 us: local(): pl.pallas_call(maxima_kernel, out_shape=[jax.ShapeDtypeStruct((docs, 1, c...]
    ppermute x3 -> x10, starting transfers between devices: 4.44 us -> 17 us  [the longest x4 10 us: other_core(): return lax.ppermute(value, AXES, pairs)]
  transfers between devices with their start and end apart: 4 -> 10, of which waited for: 4 -> 3; matrix products, arithmetic and copies ran while one was open for 1% -> 0% of each run, Pallas kernels for 0% -> 0%
where the time goes in v1:
time: 71.1 us; the launch traced here: 70.9 us
  blocking collectives  21.2 us (30%)
  Pallas kernels  20.7 us (29%)
  starting transfers between devices  17 us (24%)
  waiting for transfers between devices  7.11 us (10%)
  local copies, waits for them, and re-layouts  4.77 us (7%)
    all_to_all x1, blocking collectives, local(): mine = lax.all_to_all(copies, ('y', 'z'), 0, 0, tiled=True)  21.2 us
    pallas_call x1, Pallas kernels, local(): pl.pallas_call(maxima_kernel, out_shape=[jax.ShapeDtypeStruct((docs, 1, c...  18.1 us
    ppermute x4, starting transfers between devices, other_core(): return lax.ppermute(value, AXES, pairs)  10 us
    ppermute x3, waiting for transfers between devices, along_blk(): return lax.ppermute(value, AXES, pairs)  6.04 us
    ppermute x3, starting transfers between devices, along_x(): return lax.ppermute(value, AXES, pairs)  4.21 us
    unnamed x10, local copies, waits for them, and re-layouts  4.05 us
    ppermute x3, starting transfers between devices, along_blk(): return lax.ppermute(value, AXES, pairs)  2.81 us
    pallas_call x1, Pallas kernels, local(): pl.pallas_call(scores_kernel, out_shape=jax.ShapeDtypeStruct((docs, total...  2.61 us
  transfers between devices with their start and end apart: 10, of which 3 were waited for; matrix products, arithmetic and copies ran while one was open for 0% of the time, Pallas kernels for 0%

profile of v1, /device:TPU:1, one launch (start us, length us, event | category | flops | bytes accessed | tf_op | source)
XLA Modules:
  0.0 70.9 jit_solution(7441374601596795529)
XLA Ops:
  0.0 0.7 %broadcast_in_dim.12 = bf16[32,24,128]{2,1,0:T(8,128)(2,1)S(1)} broadcast(bf16[24,128]{1,0:T(8,128)(2,1)} %bitcast.3), dimensions={1,2} | broadcast | bytes 202752 | tf_op jit(solution)/shard_map/broadcast_in_dim | solution.py:209
  0.7 21.2 %all_to_all.5.rest_0_ = bf16[32,24,128]{2,1,0:T(8,128)(2,1)S(1)} all-to-all(bf16[32,24,128]{2,1,0:T(8,128)(2,1)S(1)} %broadcast_in_dim.12), channel_id=1, replica_groups=mesh['xh'=2,'y'=4,'xl'=2,'z'=8,'c'=2] {'y','z'}, dimensions={0} | all-to-all | bytes 393216 | tf_op jit(solution)/shard_map/all_to_all | solution.py:210
  22.0 2.7 %collective-permute-start.5 = (bf16[32,24,128]{2,1,0:T(8,128)(2,1)S(1)}, bf16[32,24,128]{2,1,0:T(8,128)(2,1)S(1)}, u32[]{:S(2)}, u32[]{:S(2)}) collective-permute-start(bf16[32,24,128]{2,1,0:T(8,128)(2,1)S(1)} %all_to_all.5.rest_0_), channel_id=1, source_target_pairs={{0,128},{1,129},{2,130},{3,131},{4,132},{5,133},{6,134},{7,135},{8... | collective-permute-start | bytes 589832 | tf_op jit(solution)/shard_map/ppermute | solution.py:33
  24.7 0.9 %collective-permute-start.3 = (bf16[32,24,128]{2,1,0:T(8,128)(2,1)S(1)}, bf16[32,24,128]{2,1,0:T(8,128)(2,1)S(1)}, u32[]{:S(2)}, u32[]{:S(2)}) collective-permute-start(bf16[32,24,128]{2,1,0:T(8,128)(2,1)S(1)} %all_to_all.5.rest_0_), channel_id=1, source_target_pairs={{0,144},{1,145},{2,146},{3,147},{4,148},{5,149},{6,150},{7,151},{8... | collective-permute-start | bytes 589832 | tf_op jit(solution)/shard_map/ppermute | solution.py:33
  25.6 0.6 collective-permute-start.1
  26.2 3.7 %collective-permute-start = (bf16[32,24,128]{2,1,0:T(8,128)(2,1)S(1)}, bf16[32,24,128]{2,1,0:T(8,128)(2,1)S(1)}, u32[]{:S(2)}, u32[]{:S(2)}) collective-permute-start(bf16[32,24,128]{2,1,0:T(8,128)(2,1)S(1)} %all_to_all.5.rest_0_), channel_id=1, source_target_pairs={{0,1},{1,0},{2,3},{3,2},{4,5},{5,4},{6,7},{7,6},{8,9},{9,8},{10,11... | collective-permute-start | bytes 589832 | tf_op jit(solution)/shard_map/ppermute | solution.py:38
  29.9 0.0 collective-permute-done.5.rest_6_
  29.9 3.1 %collective-permute-start.6 = (bf16[32,24,128]{2,1,0:T(8,128)(2,1)S(1)}, bf16[32,24,128]{2,1,0:T(8,128)(2,1)S(1)}, u32[]{:S(2)}, u32[]{:S(2)}) collective-permute-start(bf16[32,24,128]{2,1,0:T(8,128)(2,1)S(1)} %collective-permute-done.5.rest_6_), channel_id=1, source_target_pairs={{0,1},{1,0},{2,3},{3,2},{4,5},{5,4},{6,7},{7,6},{8,9},{9,8},{10,11... | collective-permute-start | bytes 589832 | tf_op jit(solution)/shard_map/ppermute | solution.py:38
  33.0 0.0 collective-permute-done.3.rest_4_
  33.0 2.1 %collective-permute-start.4 = (bf16[32,24,128]{2,1,0:T(8,128)(2,1)S(1)}, bf16[32,24,128]{2,1,0:T(8,128)(2,1)S(1)}, u32[]{:S(2)}, u32[]{:S(2)}) collective-permute-start(bf16[32,24,128]{2,1,0:T(8,128)(2,1)S(1)} %collective-permute-done.3.rest_4_), channel_id=1, source_target_pairs={{0,1},{1,0},{2,3},{3,2},{4,5},{5,4},{6,7},{7,6},{8,9},{9,8},{10,11... | collective-permute-start | bytes 589832 | tf_op jit(solution)/shard_map/ppermute | solution.py:38
  35.1 1.1 %collective-permute-start.2 = (bf16[32,24,128]{2,1,0:T(8,128)(2,1)S(1)}, bf16[32,24,128]{2,1,0:T(8,128)(2,1)S(1)}, u32[]{:S(2)}, u32[]{:S(2)}) collective-permute-start(bf16[32,24,128]{2,1,0:T(8,128)(2,1)S(1)} %collective-permute-done.1.rest_2_), channel_id=1, source_target_pairs={{0,1},{1,0},{2,3},{3,2},{4,5},{5,4},{6,7},{7,6},{8,9},{9,8},{10,11... | collective-permute-start | bytes 589832 | tf_op jit(solution)/shard_map/ppermute | solution.py:38
  36.2 1.1 %collective-permute-done.2.rest_3_ = bf16[32,24,128]{2,1,0:T(8,128)(2,1)S(1)} collective-permute-done((bf16[32,24,128]{2,1,0:T(8,128)(2,1)S(1)}, bf16[32,24,128]{2,1,0:T(8,128)(2,1)S(1)}, u32[]{:S(2)}, u32[]{:S(2)}) %collective-permute-start.2) | collective-permute-done | bytes 196640 | tf_op jit(solution)/shard_map/ppermute | solution.py:38
  37.3 1.4 %copy-done = bf16[6,1030,128]{2,1,0:T(8,128)(2,1)S(1)} copy-done((bf16[6,1030,128]{2,1,0:T(8,128)(2,1)S(1)}, bf16[6,1030,128]{2,1,0:T(8,128)(2,1)}, u32[]{:S(2)}) %copy-start) | copy-done | bytes 1582104
  38.7 0.7 copy-done.1
  39.4 0.7 copy-done.2
  40.0 0.7 copy-done.3
  40.7 0.7 copy-done.4
  41.3 18.1 %shard_map.64 = (f32[3,1,6144]{2,1,0:T(1,128)S(1)}, f32[3,1,6144]{2,1,0:T(1,128)S(1)}, f32[3,1,6144]{2,1,0:T(1,128)S(1)}, f32[3,1,6144]{2,1,0:T(1,128)S(1)}) custom-call(s32[256]{0:T(256)S(1)} %copy-done.1, s32[3]{0:T(128)S(1)} %copy-done.2, s32[3]{0:T(128)S(1)} %copy-done.3, s32[6]{0:T(128)S(1)} %copy-done.4, bf16[32,24,128]{2,1,0:T(8,128)(2,1)S(1)} %all_to_all.5.rest_0_, ...), custom_call_target="tpu_custom_call" | custom-call | tf_op jit(solution)/shard_map/pallas_call | solution.py:216
  59.4 0.5 collective-permute-start.7
  59.8 0.2 collective-permute-start.8
  60.0 2.2 %collective-permute-start.9 = (f32[3,1,6144]{2,1,0:T(1,128)S(1)}, f32[3,1,6144]{2,1,0:T(1,128)S(1)}, u32[]{:S(2)}, u32[]{:S(2)}) collective-permute-start(f32[3,1,6144]{2,1,0:T(1,128)S(1)} %get-tuple-element.12), channel_id=1, source_target_pairs={{0,29},{1,30},{2,31},{3,0},{4,1},{5,2},{6,3},{7,4},{8,5},{9,6},{10... | collective-permute-start | bytes 221192 | tf_op jit(solution)/shard_map/ppermute | solution.py:46
  62.2 1.7 %collective-permute-done.7.one_ref = f32[3,1,6144]{2,1,0:T(1,128)S(1)} collective-permute-done((f32[3,1,6144]{2,1,0:T(1,128)S(1)}, f32[3,1,6144]{2,1,0:T(1,128)S(1)}, u32[]{:S(2)}, u32[]{:S(2)}) %collective-permute-start.7) | collective-permute-done | bytes 73760 | tf_op jit(solution)/shard_map/ppermute | solution.py:46
  63.9 4.3 %collective-permute-done.9.three_ref = f32[3,1,6144]{2,1,0:T(1,128)S(1)} collective-permute-done((f32[3,1,6144]{2,1,0:T(1,128)S(1)}, f32[3,1,6144]{2,1,0:T(1,128)S(1)}, u32[]{:S(2)}, u32[]{:S(2)}) %collective-permute-start.9) | collective-permute-done | bytes 73760 | tf_op jit(solution)/shard_map/ppermute | solution.py:46
  68.2 2.6 %shard_map.65 = f32[3,256]{1,0:T(4,128)} custom-call(s32[1,256]{1,0:T(1,128)S(1)} %bitcast.2, f32[3,1,6144]{2,1,0:T(1,128)S(1)} %get-tuple-element.9.own_ref, f32[3,1,6144]{2,1,0:T(1,128)S(1)} %collective-permute-done.7.one_ref, f32[3,1,6144]{2,1,0:T(1,128)S(1)} %collective-permute-done.8.two_ref, f32[3,1,6144]{2,1,0:T(1,128)S(1)} %collective-permute-done.9.three_ref), custom_call_target="tpu_custom_call" | custom-call | tf_op jit(solution)/shard_map/pallas_call | solution.py:230
  (10 shorter events, 0.0 us)
Async XLA Ops:
  22.0 7.9 %collective-permute-start.5 = (bf16[32,24,128]{2,1,0:T(8,128)(2,1)S(1)}, bf16[32,24,128]{2,1,0:T(8,128)(2,1)S(1)}, u32[]{:S(2)}, u32[]{:S(2)}) collective-permute-start(bf16[32,24,128]{2,1,0:T(8,128)(2,1)S(1)} %all_to_all.5.rest_0_), channel_id=1, source_target_pairs={{0,128},{1,129},{2,130},{3,131},{4,132},{5,133},{6,134},{7,135},{8... | collective-permute-start | bytes 589832 | tf_op jit(solution)/shard_map/ppermute | solution.py:33
  24.7 8.3 %collective-permute-start.3 = (bf16[32,24,128]{2,1,0:T(8,128)(2,1)S(1)}, bf16[32,24,128]{2,1,0:T(8,128)(2,1)S(1)}, u32[]{:S(2)}, u32[]{:S(2)}) collective-permute-start(bf16[32,24,128]{2,1,0:T(8,128)(2,1)S(1)} %all_to_all.5.rest_0_), channel_id=1, source_target_pairs={{0,144},{1,145},{2,146},{3,147},{4,148},{5,149},{6,150},{7,151},{8... | collective-permute-start | bytes 589832 | tf_op jit(solution)/shard_map/ppermute | solution.py:33
  25.6 9.6 %collective-permute-start.1 = (bf16[32,24,128]{2,1,0:T(8,128)(2,1)S(1)}, bf16[32,24,128]{2,1,0:T(8,128)(2,1)S(1)}, u32[]{:S(2)}, u32[]{:S(2)}) collective-permute-start(bf16[32,24,128]{2,1,0:T(8,128)(2,1)S(1)} %all_to_all.5.rest_0_), channel_id=1, source_target_pairs={{0,16},{1,17},{2,18},{3,19},{4,20},{5,21},{6,22},{7,23},{8,24},{9,... | collective-permute-start | bytes 589832 | tf_op jit(solution)/shard_map/ppermute | solution.py:33
  26.2 10.0 %collective-permute-start = (bf16[32,24,128]{2,1,0:T(8,128)(2,1)S(1)}, bf16[32,24,128]{2,1,0:T(8,128)(2,1)S(1)}, u32[]{:S(2)}, u32[]{:S(2)}) collective-permute-start(bf16[32,24,128]{2,1,0:T(8,128)(2,1)S(1)} %all_to_all.5.rest_0_), channel_id=1, source_target_pairs={{0,1},{1,0},{2,3},{3,2},{4,5},{5,4},{6,7},{7,6},{8,9},{9,8},{10,11... | collective-permute-start | bytes 589832 | tf_op jit(solution)/shard_map/ppermute | solution.py:38
  29.9 6.3 %collective-permute-start.6 = (bf16[32,24,128]{2,1,0:T(8,128)(2,1)S(1)}, bf16[32,24,128]{2,1,0:T(8,128)(2,1)S(1)}, u32[]{:S(2)}, u32[]{:S(2)}) collective-permute-start(bf16[32,24,128]{2,1,0:T(8,128)(2,1)S(1)} %collective-permute-done.5.rest_6_), channel_id=1, source_target_pairs={{0,1},{1,0},{2,3},{3,2},{4,5},{5,4},{6,7},{7,6},{8,9},{9,8},{10,11... | collective-permute-start | bytes 589832 | tf_op jit(solution)/shard_map/ppermute | solution.py:38
  33.0 3.2 %collective-permute-start.4 = (bf16[32,24,128]{2,1,0:T(8,128)(2,1)S(1)}, bf16[32,24,128]{2,1,0:T(8,128)(2,1)S(1)}, u32[]{:S(2)}, u32[]{:S(2)}) collective-permute-start(bf16[32,24,128]{2,1,0:T(8,128)(2,1)S(1)} %collective-permute-done.3.rest_4_), channel_id=1, source_target_pairs={{0,1},{1,0},{2,3},{3,2},{4,5},{5,4},{6,7},{7,6},{8,9},{9,8},{10,11... | collective-permute-start | bytes 589832 | tf_op jit(solution)/shard_map/ppermute | solution.py:38
  35.1 2.1 %collective-permute-start.2 = (bf16[32,24,128]{2,1,0:T(8,128)(2,1)S(1)}, bf16[32,24,128]{2,1,0:T(8,128)(2,1)S(1)}, u32[]{:S(2)}, u32[]{:S(2)}) collective-permute-start(bf16[32,24,128]{2,1,0:T(8,128)(2,1)S(1)} %collective-permute-done.1.rest_2_), channel_id=1, source_target_pairs={{0,1},{1,0},{2,3},{3,2},{4,5},{5,4},{6,7},{7,6},{8,9},{9,8},{10,11... | collective-permute-start | bytes 589832 | tf_op jit(solution)/shard_map/ppermute | solution.py:38
  37.3 1.4 %copy-start = (bf16[6,1030,128]{2,1,0:T(8,128)(2,1)S(1)}, bf16[6,1030,128]{2,1,0:T(8,128)(2,1)}, u32[]{:S(2)}) copy-start(bf16[6,1030,128]{2,1,0:T(8,128)(2,1)} %rest_8_.1) | copy-start | bytes 4746244
  38.7 0.7 copy-start.1
  39.4 0.7 copy-start.2
  40.0 0.7 copy-start.3
  40.7 0.7 copy-start.4
  59.4 4.5 %collective-permute-start.7 = (f32[3,1,6144]{2,1,0:T(1,128)S(1)}, f32[3,1,6144]{2,1,0:T(1,128)S(1)}, u32[]{:S(2)}, u32[]{:S(2)}) collective-permute-start(f32[3,1,6144]{2,1,0:T(1,128)S(1)} %get-tuple-element.10), channel_id=1, source_target_pairs={{0,31},{1,0},{2,1},{3,2},{4,3},{5,4},{6,5},{7,6},{8,7},{9,8},{10,9... | collective-permute-start | bytes 221192 | tf_op jit(solution)/shard_map/ppermute | solution.py:46
  59.8 4.0 %collective-permute-start.8 = (f32[3,1,6144]{2,1,0:T(1,128)S(1)}, f32[3,1,6144]{2,1,0:T(1,128)S(1)}, u32[]{:S(2)}, u32[]{:S(2)}) collective-permute-start(f32[3,1,6144]{2,1,0:T(1,128)S(1)} %get-tuple-element.11), channel_id=1, source_target_pairs={{0,30},{1,31},{2,0},{3,1},{4,2},{5,3},{6,4},{7,5},{8,6},{9,7},{10,... | collective-permute-start | bytes 221192 | tf_op jit(solution)/shard_map/ppermute | solution.py:46
  60.0 8.2 %collective-permute-start.9 = (f32[3,1,6144]{2,1,0:T(1,128)S(1)}, f32[3,1,6144]{2,1,0:T(1,128)S(1)}, u32[]{:S(2)}, u32[]{:S(2)}) collective-permute-start(f32[3,1,6144]{2,1,0:T(1,128)S(1)} %get-tuple-element.12), channel_id=1, source_target_pairs={{0,29},{1,30},{2,31},{3,0},{4,1},{5,2},{6,3},{7,4},{8,5},{9,6},{10... | collective-permute-start | bytes 221192 | tf_op jit(solution)/shard_map/ppermute | solution.py:46

commit v2 on v0

v2 whole, which is shorter than its diff:
```python
import functools

import jax
import jax.numpy as jnp
from jax import lax
from jax.experimental import pallas as pl
from jax.experimental.pallas import tpu as pltpu
from jax.sharding import Mesh, PartitionSpec as P

SPILL = 3
SIZES = (2, 4, 2, 8, 2)
AXES = ("xh", "y", "xl", "z", "c")
NX, NY, NZ, NC = 4, 4, 8, 2
CHUNK = NY * NZ
TILE = 256
lowest = -1e30
VMEM_LIMIT = 48 * 1024 * 1024
TRANSPOSED = (((1,), (1,)), ((), ()))


def device_id(x, y, z, c):
    return (((x // 2) * NY + y) * 2 + x % 2) * NZ * NC + z * NC + c


def coordinates():
    return [
        (x, y, z, c) for x in range(NX) for y in range(NY) for z in range(NZ) for c in range(NC)
    ]


def along_x(value, steps):
    pairs = [
        (device_id(x, y, z, c), device_id((x + steps) % NX, y, z, c)) for x, y, z, c in coordinates()
    ]
    return lax.ppermute(value, AXES, pairs)


def other_core(value):
    pairs = [(device_id(x, y, z, c), device_id(x, y, z, 1 - c)) for x, y, z, c in coordinates()]
    return lax.ppermute(value, AXES, pairs)


def along_blk(value, steps):
    count = 32
    pairs = [
        (g * count + b, g * count + (b + steps) % count) for g in range(8) for b in range(count)
    ]
    return lax.ppermute(value, AXES, pairs)


def region_of(x_abs, core):
    return (x_abs // 2) * (NY * 2 * NZ * NC) + (x_abs % 2) * (NZ * NC) + core


PLACES = [y * (2 * NZ * NC) + z * NC for y in range(NY) for z in range(NZ)]


def chunk_total(len_ref, x_abs, core):
    first = region_of(x_abs, core)
    terms = [len_ref[first + place] for place in PLACES]
    while len(terms) > 1:
        terms = [sum(terms[i : i + 2]) for i in range(0, len(terms), 2)]
    return terms[0]


def chunk_of(spec, x, c):
    steps, core = spec
    return lax.rem(x + NX - steps, NX), (c if core == 0 else 1 - c)


def compact(len_ref, live_ref, base, chunk, source):
    tokens = source.shape[1]
    first = region_of(*chunk)
    at = base
    for k, place in enumerate(PLACES):
        live_ref[pl.ds(at, tokens), :] = source[k].astype(jnp.float32)
        at = at + len_ref[first + place]
    return at - base


def slot_ids(count_ref, offset_ref, helper_ref, pages):
    docs = count_ref.shape[0]
    ids = []
    for k in pages:
        slot = jnp.int32(0) if helper_ref is None else helper_ref[k]
        for j in range(docs):
            inside = (offset_ref[j] <= k) & (k < offset_ref[j] + count_ref[j])
            slot = jnp.where(inside, j, slot)
        ids.append(jnp.clip(slot, 0, (SPILL + 1) * docs - 1))
    return ids


def fill_tails(pages_ref, tail_ref):
    pages, patches, _ = pages_ref.shape
    whole = patches // 16 * 16
    tail_ref[...] = jnp.zeros(tail_ref.shape, jnp.float32)
    for p in range(pages):
        tail_ref[8 * p : 8 * p + patches - whole, :] = pages_ref[p, whole:, :].astype(jnp.float32)
        for extra in range(patches - whole, 8):
            tail_ref[8 * p + extra : 8 * p + extra + 1, :] = pages_ref[
                p, patches - 1 : patches, :
            ].astype(jnp.float32)
    return tail_ref[...].astype(jnp.bfloat16)


def page_best(token_rows, pages_ref, tails):
    pages, patches, _ = pages_ref.shape
    whole = patches // 16 * 16
    columns = token_rows.shape[0]
    tail_scores = lax.dot_general(
        tails, token_rows, TRANSPOSED, preferred_element_type=jnp.float32
    )
    rows = []
    for p in range(pages):
        scores = lax.dot_general(
            pages_ref[p, :whole, :], token_rows, TRANSPOSED, preferred_element_type=jnp.float32
        )
        best = jnp.max(scores.reshape(whole // 8, 8, columns), axis=0)
        best = jnp.maximum(best, tail_scores[8 * p : 8 * p + 8])
        rows.append(jnp.max(best, axis=0, keepdims=True))
    return rows


def over_tiles(total, visit):
    tiles = (total + TILE - 1) // TILE

    def double(i, _):
        visit(pl.multiple_of(i * (2 * TILE), 2 * TILE), 2 * TILE)
        return 0

    lax.fori_loop(0, tiles // 2, double, 0)

    @pl.when(tiles % 2 == 1)
    def _():
        visit(pl.multiple_of((tiles - 1) * TILE, TILE), TILE)


def own_position():
    return lax.axis_index("xh") * 2 + lax.axis_index("xl"), lax.axis_index("c")


def all_slots(live_ref, base, at, size, ids, pages_ref, tails, slot_ref, outs, write):
    token_rows = live_ref[pl.ds(base + at, size), :].astype(jnp.bfloat16)
    slot_ref[...] = jnp.full(slot_ref.shape, lowest, jnp.float32)
    for slot, best in zip(ids, page_best(token_rows, pages_ref, tails)):
        slot_ref[slot, :, :size] = jnp.maximum(slot_ref[slot, :, :size], best)
    docs = outs[0].shape[0]
    for distance in range(SPILL + 1):
        for j in range(docs):
            write(outs[distance], j, slot_ref[distance * docs + j, :, :size])
    return token_rows


def whole_chunks(specs, plan_ref, sources, outs, pages_ref, live_ref, slot_ref, ids, tails):
    x, c = own_position()
    room = live_ref.shape[0] // len(specs)
    totals = [
        compact(plan_ref, live_ref, i * room, chunk_of(spec, x, c), source)
        for i, (spec, source) in enumerate(zip(specs, sources))
    ]
    for i in range(len(specs)):

        def visit(at, size, i=i):
            def write(out, j, value):
                out[j, i, :, pl.ds(at, size)] = value

            all_slots(live_ref, i * room, at, size, ids, pages_ref, tails, slot_ref, outs, write)

        over_tiles(totals[i], visit)


def first_kernel(specs, len_hbm, count_hbm, offset_hbm, helper_hbm, *rest):
    sources, rest = rest[: len(specs)], rest[len(specs) :]
    pages_ref, rest = rest[0], rest[1:]
    outs, rest = rest[: SPILL + 1], rest[SPILL + 1 :]
    plan_ref, count_ref, offset_ref, helper_ref, live_ref, tail_ref, slot_ref, sem = rest
    pages = pages_ref.shape[0]
    moves = [
        pltpu.make_async_copy(source, target, sem.at[i])
        for i, (source, target) in enumerate(
            (
                (len_hbm, plan_ref.at[pl.ds(0, len_hbm.shape[0])]),
                (count_hbm, count_ref),
                (offset_hbm, offset_ref),
                (helper_hbm, helper_ref),
            )
        )
    ]
    for move in moves:
        move.start()
    tails = fill_tails(pages_ref, tail_ref)
    for move in moves:
        move.wait()
    ids = slot_ids(count_ref, offset_ref, helper_ref, range(pages))
    at = len_hbm.shape[0]
    for k in range(pages):
        plan_ref[at + k] = ids[k]
    for chunk in range(NX * NC):
        plan_ref[at + pages + chunk] = chunk_total(plan_ref, chunk // NC, chunk % NC)
    whole_chunks(specs, plan_ref, sources, outs, pages_ref, live_ref, slot_ref, ids, tails)


def more_kernel(specs, queries, plan_ref, *rest):
    sources, rest = rest[: len(specs)], rest[len(specs) :]
    pages_ref, rest = rest[0], rest[1:]
    outs, rest = rest[: SPILL + 1], rest[SPILL + 1 :]
    live_ref, tail_ref, slot_ref = rest
    ids = [plan_ref[queries + k] for k in range(pages_ref.shape[0])]
    tails = fill_tails(pages_ref, tail_ref)
    whole_chunks(specs, plan_ref, sources, outs, pages_ref, live_ref, slot_ref, ids, tails)


def chunk_count(plan_ref, chunk):
    return plan_ref[plan_ref.shape[0] - NX * NC + chunk[0] * NC + chunk[1]]


def most_tokens(plan_ref):
    most = plan_ref[plan_ref.shape[0] - NX * NC]
    for chunk in range(1, NX * NC):
        most = jnp.maximum(most, plan_ref[plan_ref.shape[0] - NX * NC + chunk])
    return most


def chosen_kernel(plan_ref, lens_ref, chosen_ref):
    span = chosen_ref.shape[0] // (NX * NC)
    half = chosen_ref.shape[1]
    starts, ends = query_columns(lens_ref[...], span)

    def step(tile, _):
        for chunk in range(NX * NC):
            lanes = slice(chunk // (2 * NC) * half, (chunk // (2 * NC) + 1) * half)
            first = pl.multiple_of(chunk * span + tile * TILE, TILE)
            token = lax.broadcasted_iota(jnp.int32, (TILE, half), 0) + first
            inside = (token >= starts[:, lanes]) & (token < ends[:, lanes])
            chosen_ref[pl.ds(first, TILE), :] = jnp.where(inside, 1.0, 0.0).astype(jnp.bfloat16)
        return 0

    lax.fori_loop(0, (most_tokens(plan_ref) + TILE - 1) // TILE, step, 0)


def query_columns(lens, span):
    queries = lens.shape[1]

    def chunk(n):
        return ((n // (NC * NZ * 2 * NY)) * 2 + (n // (NC * NZ)) % 2) * NC + n % NC

    def place(n):
        return (n // (NC * NZ * 2)) % NY * NZ + (n // NC) % NZ

    one = lax.broadcasted_iota(jnp.int32, (queries, queries), 0)
    two = lax.broadcasted_iota(jnp.int32, (queries, queries), 1)
    before = (chunk(one) == chunk(two)) & (place(one) < place(two))
    row = jnp.broadcast_to(lens.astype(jnp.float32).astype(jnp.bfloat16), (16, queries))
    starts = jnp.dot(
        row,
        jnp.where(before, 1.0, 0.0).astype(jnp.bfloat16),
        preferred_element_type=jnp.float32,
    )[0:1].astype(jnp.int32)
    starts = starts + chunk(lax.broadcasted_iota(jnp.int32, (1, queries), 1)) * span
    return starts, starts + lens


def late_kernel(specs, placed, queries, plan_ref, *rest):
    sources, rest = rest[: len(specs)], rest[len(specs) :]
    all_pages_ref, rest = rest[0], rest[1:]
    before, rest = rest[: len(placed) * (SPILL + 1)], rest[len(placed) * (SPILL + 1) :]
    outs, rest = rest[: SPILL + 1], rest[SPILL + 1 :]
    kept_ref, live_ref, tail_ref, slot_ref = rest
    docs = outs[0].shape[0]
    pages = all_pages_ref.shape[0]
    pages_ref = all_pages_ref.at[pl.ds(docs, pages - docs)]
    x, c = own_position()
    room = kept_ref.shape[1]
    span = outs[0].shape[2] // (NX * NC)

    def column(spec):
        chunk = chunk_of(spec, x, c)
        return pl.multiple_of((chunk[0] * NC + chunk[1]) * span, TILE)

    for group, group_specs in enumerate(placed):
        for i, spec in enumerate(group_specs):
            for distance in range(SPILL + 1):
                for j in range(docs):
                    outs[distance][j, :, pl.ds(column(spec), span)] = before[
                        group * (SPILL + 1) + distance
                    ][j, i]
    ids = [plan_ref[queries + k] for k in range(docs, pages)]
    tails = fill_tails(pages_ref, tail_ref)
    totals = [
        compact(plan_ref, live_ref, i * room, chunk_of(spec, x, c), source)
        for i, (spec, source) in enumerate(zip(specs, sources))
    ]
    for i, spec in enumerate(specs):
        where = column(spec)

        def visit(at, size, i=i, where=where):
            to = pl.multiple_of(where + at, TILE)

            def write(out, j, value):
                out[j, :, pl.ds(to, size)] = value

            kept_ref[i, pl.ds(at, size), :] = all_slots(
                live_ref, i * room, at, size, ids, pages_ref, tails, slot_ref, outs, write
            )

        over_tiles(totals[i], visit)


def home_kernel(specs, queries, plan_ref, kept_ref, all_pages_ref, before_ref, out_ref, tail_ref):
    docs, _, _, span = out_ref.shape
    pages_ref = all_pages_ref.at[pl.ds(0, docs)]
    x, c = own_position()
    ids = [plan_ref[queries + k] for k in range(docs)]
    tails = fill_tails(pages_ref, tail_ref)
    for i, spec in enumerate(specs):
        chunk = chunk_of(spec, x, c)
        where = pl.multiple_of((chunk[0] * NC + chunk[1]) * span, TILE)

        def visit(at, size, i=i, where=where):
            to = pl.multiple_of(where + at, TILE)
            rows = page_best(kept_ref[i, pl.ds(at, size), :], pages_ref, tails)
            for j in range(docs):
                out_ref[j, i, :, pl.ds(at, size)] = before_ref[j, :, pl.ds(to, size)]
            for slot, best in zip(ids, rows):
                out_ref[slot, i, :, pl.ds(at, size)] = jnp.maximum(
                    out_ref[slot, i, :, pl.ds(at, size)], best
                )

        over_tiles(chunk_count(plan_ref, chunk), visit)


def scores_kernel(groups, plan_ref, lens_ref, chosen_ref, *rest):
    homes, rest = rest[: len(groups)], rest[len(groups) :]
    received, (out_ref, acc_ref) = rest[:SPILL], rest[SPILL:]
    docs, _, columns_all = received[0].shape
    lens = lens_ref[...]
    span = columns_all // (NX * NC)
    x, c = own_position()
    acc_ref[...] = jnp.zeros(acc_ref.shape, jnp.float32)
    parts_list = [
        (home, i, chunk_of(spec, x, c))
        for home, group in zip(homes, groups)
        for i, spec in enumerate(group)
    ]

    def visit(at, size):
        for home_ref, i, chunk in parts_list:
            to = pl.multiple_of((chunk[0] * NC + chunk[1]) * span + at, TILE)
            total = chunk_count(plan_ref, chunk)
            live = lax.broadcasted_iota(jnp.int32, (1, size), 1) + at < total
            parts = []
            for j in range(docs):
                value = home_ref[j, i, :, pl.ds(at, size)]
                for ref in received:
                    value = jnp.maximum(value, ref[j, :, pl.ds(to, size)])
                value = jnp.where(live, value, 0.0)
                high = value.astype(jnp.bfloat16).astype(jnp.float32)
                left = value - high
                middle = left.astype(jnp.bfloat16).astype(jnp.float32)
                parts += [high, middle, left - middle]
            parts.append(jnp.zeros((acc_ref.shape[1] - len(parts), size), jnp.float32))
            left_side = jnp.concatenate(parts, axis=0).astype(jnp.bfloat16)
            x_hi = chunk[0] // 2
            acc_ref[x_hi] = acc_ref[x_hi] + jnp.dot(
                left_side, chosen_ref[pl.ds(to, size), :], preferred_element_type=jnp.float32
            )

    over_tiles(most_tokens(plan_ref), visit)
    half = acc_ref.shape[2]
    for x_hi in range(acc_ref.shape[0]):
        lanes = slice(x_hi * half, (x_hi + 1) * half)
        divisor = lens[:, lanes].astype(jnp.float32)
        for j in range(docs):
            high, middle, low = (acc_ref[x_hi, 3 * j + i : 3 * j + i + 1, :] for i in range(3))
            out_ref[j : j + 1, lanes] = ((high + middle) + low) / divisor


SMEM = pl.BlockSpec(memory_space=pltpu.SMEM)
VMEM = pl.BlockSpec(memory_space=pltpu.VMEM)
HBM = pl.BlockSpec(memory_space=pltpu.HBM)


def copies_kernel(block_ref, out_ref):
    for i in range(out_ref.shape[0]):
        out_ref[i] = block_ref[0]


def local(queries, query_len, pages, page_count, page_offset, helper_doc):
    docs = page_count.shape[0]
    total = query_len.shape[0]
    tokens, width = queries.shape[1:]
    columns = total * tokens
    span = columns // (NX * NC)
    room = span + TILE
    params = pltpu.CompilerParams(vmem_limit_bytes=VMEM_LIMIT)
    whole = [jax.ShapeDtypeStruct((docs, 1, columns), jnp.float32)] * (SPILL + 1)
    slots = pltpu.VMEM(((SPILL + 1) * docs, 1, 2 * TILE), jnp.float32)
    row = query_len[None, :]
    own, far, rest = [(0, 0), (0, 1)], [(2, 0)], [(2, 1), (1, 0), (1, 1), (3, 0), (3, 1)]

    def part(specs):
        return [jax.ShapeDtypeStruct((docs, len(specs), 1, span), jnp.float32)] * (SPILL + 1)

    def tail_room(count):
        return pltpu.VMEM((8 * count + 8 * count % 16, width), jnp.float32)

    def live_room(specs):
        return pltpu.VMEM((len(specs) * room, width), jnp.float32)

    def cost(rows):
        return pl.CostEstimate(
            flops=2 * rows * columns * width, bytes_accessed=rows * width * 2, transcendentals=0
        )

    copies = pl.pallas_call(
        copies_kernel,
        out_shape=jax.ShapeDtypeStruct((CHUNK, tokens, width), jnp.bfloat16),
        in_specs=[VMEM],
        out_specs=VMEM,
        cost_estimate=cost(pages.shape[0] * pages.shape[1]),
    )(queries)
    mine = lax.all_to_all(copies, ("y", "z"), 0, 0, tiled=True)
    mine_other = other_core(mine)
    two, one, three = [along_x(mine, steps) for steps in (2, 1, 3)]

    *own_out, plan = pl.pallas_call(
        functools.partial(first_kernel, own),
        out_shape=part(own)
        + [jax.ShapeDtypeStruct((total + pages.shape[0] + NX * NC,), jnp.int32)],
        in_specs=[HBM] * 4 + [VMEM] * (len(own) + 1),
        out_specs=[VMEM] * (SPILL + 1) + [SMEM],
        scratch_shapes=[
            pltpu.SMEM(page_count.shape, jnp.int32),
            pltpu.SMEM(page_offset.shape, jnp.int32),
            pltpu.SMEM(helper_doc.shape, jnp.int32),
            live_room(own),
            tail_room(pages.shape[0]),
            slots,
            pltpu.SemaphoreType.DMA((4,)),
        ],
        compiler_params=params,
        cost_estimate=cost(700),
    )(query_len, page_count, page_offset, helper_doc, mine, mine_other, pages)

    two, plan = lax.optimization_barrier((two, plan))
    far_out = pl.pallas_call(
        functools.partial(more_kernel, far, total),
        out_shape=part(far),
        in_specs=[SMEM] + [VMEM] * (len(far) + 1),
        out_specs=[VMEM] * (SPILL + 1),
        scratch_shapes=[live_room(far), tail_room(pages.shape[0]), slots],
        compiler_params=params,
        cost_estimate=cost(700),
    )(plan, two, pages)

    one, two, three, far_out = lax.optimization_barrier((one, two, three, far_out))
    two_other, one_other, three_other = [other_core(value) for value in (two, one, three)]
    chosen = pl.pallas_call(
        chosen_kernel,
        out_shape=jax.ShapeDtypeStruct((columns, total // 2), jnp.bfloat16),
        in_specs=[SMEM, VMEM],
        out_specs=VMEM,
        compiler_params=params,
        cost_estimate=cost(pages.shape[1]),
    )(plan, row)
    arrived = [two_other, one, one_other, three, three_other]
    *arrived, chosen = lax.optimization_barrier((*arrived, chosen))

    *partials, kept = pl.pallas_call(
        functools.partial(late_kernel, rest, (own, far), total),
        out_shape=whole + [jax.ShapeDtypeStruct((len(rest), room, width), jnp.bfloat16)],
        in_specs=[SMEM] + [VMEM] * (len(rest) + 1 + 2 * (SPILL + 1)),
        out_specs=[VMEM] * (SPILL + 2),
        scratch_shapes=[live_room(rest), tail_room(pages.shape[0] - docs), slots],
        compiler_params=params,
        cost_estimate=cost((pages.shape[0] - docs) * pages.shape[1]),
    )(plan, *arrived, pages, *own_out, *far_out)
    received = [along_blk(partials[distance], -distance) for distance in range(1, SPILL + 1)]

    rest_home = pl.pallas_call(
        functools.partial(home_kernel, rest, total),
        out_shape=part(rest)[0],
        in_specs=[SMEM] + [VMEM] * 3,
        out_specs=VMEM,
        scratch_shapes=[tail_room(docs)],
        compiler_params=params,
        cost_estimate=cost(docs * pages.shape[1]),
    )(plan, kept, pages, partials[0])

    return pl.pallas_call(
        functools.partial(scores_kernel, (own, far, rest)),
        out_shape=jax.ShapeDtypeStruct((docs, total), jnp.float32),
        in_specs=[SMEM] + [VMEM] * (SPILL + 5),
        out_specs=VMEM,
        scratch_shapes=[pltpu.VMEM((2, 16, total // 2), jnp.float32)],
        compiler_params=params,
    )(plan, row, chosen, own_out[0], far_out[0], rest_home, *received)


def solution(mesh):
    split = Mesh(mesh.devices.reshape(SIZES), AXES)
    return jax.shard_map(
        local,
        mesh=split,
        in_specs=(P(AXES, None, None), P(), P(AXES, None, None), P(AXES), P(AXES), P(AXES)),
        out_specs=P(AXES, None),
        check_vma=False,
    )
```

time: 468 us -> 57.9 us (0.12)
  waiting for transfers between devices: 415 us -> 0.33 us
  matrix products: 30.1 us -> 0 us
  Pallas kernels: 0 us -> 24.3 us
  blocking collectives: 0 us -> 21.4 us
  between operations: 13.4 us -> 0.14 us
  starting transfers between devices: 4.44 us -> 11.5 us
    all_gather x1 -> x0, waiting for transfers between devices: 406 us -> none  [local(): lax.all_gather(queries, ('group', 'blk'), axis=0, tiled=True)]
    dot_general x6 -> x0, matrix products: 30.1 us -> none  [visit(): lax.dot_general(page_rows, token_rows, (((1,), (1,)), ((), ())), preferre...]
    pallas_call x0 -> x7, Pallas kernels: none -> 24.3 us  [the longest x1 6.15 us: local(): pl.pallas_call(functools.partial(late_kernel, rest, (own, far), total), o...]
    all_to_all x0 -> x1, blocking collectives: none -> 21.4 us  [local(): mine = lax.all_to_all(copies, ('y', 'z'), 0, 0, tiled=True)]
    ppermute x3 -> x10, waiting for transfers between devices: 7.5 us -> 0.33 us  [the longest x3 0.29 us: along_x(): return lax.ppermute(value, AXES, pairs)]
    ppermute x3 -> x10, starting transfers between devices: 4.44 us -> 11.5 us  [the longest x3 4.21 us: along_x(): return lax.ppermute(value, AXES, pairs)]
  transfers between devices with their start and end apart: 4 -> 10, of which waited for: 4 -> 1; matrix products, arithmetic and copies ran while one was open for 1% -> 0% of each run, Pallas kernels for 0% -> 26%
where the time goes in v2:
time: 57.9 us; the launch traced here: 57.7 us
  Pallas kernels  24.3 us (42%)
  blocking collectives  21.4 us (37%)
  starting transfers between devices  11.5 us (20%)
    all_to_all x1, blocking collectives, local(): mine = lax.all_to_all(copies, ('y', 'z'), 0, 0, tiled=True)  21.4 us
    pallas_call x1, Pallas kernels, local(): pl.pallas_call(functools.partial(late_kernel, rest, (own, far), total), o...  6.15 us
    pallas_call x1, Pallas kernels, local(): pl.pallas_call(functools.partial(home_kernel, rest, total), out_shape=par...  6.13 us
    pallas_call x1, Pallas kernels, local(): pl.pallas_call(functools.partial(first_kernel, own), out_shape=part(own)...  5.31 us
    ppermute x3, starting transfers between devices, along_x(): return lax.ppermute(value, AXES, pairs)  4.21 us
    ppermute x4, starting transfers between devices, other_core(): return lax.ppermute(value, AXES, pairs)  4.2 us
    ppermute x3, starting transfers between devices, along_blk(): return lax.ppermute(value, AXES, pairs)  3.04 us
    pallas_call x1, Pallas kernels, local(): pl.pallas_call(functools.partial(more_kernel, far, total), out_shape=part...  2.51 us
  transfers between devices with their start and end apart: 10, of which 1 were waited for; matrix products, arithmetic and copies ran while one was open for 0% of the time, Pallas kernels for 26%

profile of v2, /device:TPU:1, one launch (start us, length us, event | category | flops | bytes accessed | tf_op | source)
XLA Modules:
  0.0 57.7 jit_solution(2253150849628728022)
XLA Ops:
  0.0 1.5 %shard_map.64 = bf16[32,24,128]{2,1,0:T(8,128)(2,1)} custom-call(bf16[1,24,128]{2,1,0:T(8,128)(2,1)} %block_ref.1), custom_call_target="tpu_custom_call" | custom-call | flops 9720299520 | bytes 1582080 | tf_op jit(solution)/shard_map/pallas_call | solution.py:415
  1.5 21.4 %all_to_all.5.rest_0_ = bf16[32,24,128]{2,1,0:T(8,128)(2,1)S(1)} all-to-all(bf16[32,24,128]{2,1,0:T(8,128)(2,1)} %shard_map.64), channel_id=1, replica_groups=mesh['xh'=2,'y'=4,'xl'=2,'z'=8,'c'=2] {'y','z'}, dimensions={0} | all-to-all | bytes 393216 | tf_op jit(solution)/shard_map/all_to_all | solution.py:422
  23.0 2.8 %collective-permute-start.1 = (bf16[32,24,128]{2,1,0:T(8,128)(2,1)S(1)}, bf16[32,24,128]{2,1,0:T(8,128)(2,1)S(1)}, u32[]{:S(2)}, u32[]{:S(2)}) collective-permute-start(bf16[32,24,128]{2,1,0:T(8,128)(2,1)S(1)} %all_to_all.5.rest_0_), channel_id=1, source_target_pairs={{0,1},{1,0},{2,3},{3,2},{4,5},{5,4},{6,7},{7,6},{8,9},{9,8},{10,11... | collective-permute-start | bytes 589832 | tf_op jit(solution)/shard_map/ppermute | solution.py:40
  25.8 2.7 %collective-permute-start = (bf16[32,24,128]{2,1,0:T(8,128)(2,1)S(1)}, bf16[32,24,128]{2,1,0:T(8,128)(2,1)S(1)}, u32[]{:S(2)}, u32[]{:S(2)}) collective-permute-start(bf16[32,24,128]{2,1,0:T(8,128)(2,1)S(1)} %all_to_all.5.rest_0_), channel_id=1, source_target_pairs={{0,128},{1,129},{2,130},{3,131},{4,132},{5,133},{6,134},{7,135},{8... | collective-permute-start | bytes 589832 | tf_op jit(solution)/shard_map/ppermute | solution.py:35
  28.6 0.9 %collective-permute-start.3 = (bf16[32,24,128]{2,1,0:T(8,128)(2,1)S(1)}, bf16[32,24,128]{2,1,0:T(8,128)(2,1)S(1)}, u32[]{:S(2)}, u32[]{:S(2)}) collective-permute-start(bf16[32,24,128]{2,1,0:T(8,128)(2,1)S(1)} %all_to_all.5.rest_0_), channel_id=1, source_target_pairs={{0,144},{1,145},{2,146},{3,147},{4,148},{5,149},{6,150},{7,151},{8... | collective-permute-start | bytes 589832 | tf_op jit(solution)/shard_map/ppermute | solution.py:35
  29.4 0.6 %collective-permute-start.2 = (bf16[32,24,128]{2,1,0:T(8,128)(2,1)S(1)}, bf16[32,24,128]{2,1,0:T(8,128)(2,1)S(1)}, u32[]{:S(2)}, u32[]{:S(2)}) collective-permute-start(bf16[32,24,128]{2,1,0:T(8,128)(2,1)S(1)} %all_to_all.5.rest_0_), channel_id=1, source_target_pairs={{0,16},{1,17},{2,18},{3,19},{4,20},{5,21},{6,22},{7,23},{8,24},{9,... | collective-permute-start | bytes 589832 | tf_op jit(solution)/shard_map/ppermute | solution.py:35
  30.1 5.3 %shard_map.65 = (f32[3,2,1,768]{3,2,1,0:T(1,128)S(1)}, f32[3,2,1,768]{3,2,1,0:T(1,128)S(1)}, f32[3,2,1,768]{3,2,1,0:T(1,128)S(1)}, f32[3,2,1,768]{3,2,1,0:T(1,128)S(1)}, s32[270]{0:T(512)S(1)}) custom-call(s32[256]{0:T(256)S(1)} %copy-done, s32[3]{0:T(128)S(1)} %copy-done.2, s32[3]{0:T(128)S(1)} %copy-done.3, s32[6]{0:T(128)S(1)} %copy-done.4, ...), custom_call_target="tpu_custom_call" | custom-call | flops 1101004800 | bytes 179200 | tf_op jit(solution)/shard_map/pallas_call | solution.py:426
  35.4 0.0 collective-permute-done.rest_0_
  35.4 2.5 %shard_map.66 = (f32[3,1,1,768]{3,2,1,0:T(1,128)S(1)}, f32[3,1,1,768]{3,2,1,0:T(1,128)S(1)}, f32[3,1,1,768]{3,2,1,0:T(1,128)S(1)}, f32[3,1,1,768]{3,2,1,0:T(1,128)S(1)}) custom-call(s32[270]{0:T(512)S(1)} %get-tuple-element.35.plan_ref, bf16[32,24,128]{2,1,0:T(8,128)(2,1)S(1)} %collective-permute-done.rest_0_, bf16[6,1030,128]{2,1,0:T(8,128)(2,1)S(1)} %copy-done.1), custom_call_target="tpu_custom_call" | custom-call | flops 1101004800 | bytes 179200 | tf_op jit(solution)/shard_map/pallas_call | solution.py:446
  37.9 0.3 collective-permute-done.3.rest_3_
  38.2 0.8 %collective-permute-start.4 = (bf16[32,24,128]{2,1,0:T(8,128)(2,1)S(1)}, bf16[32,24,128]{2,1,0:T(8,128)(2,1)S(1)}, u32[]{:S(2)}, u32[]{:S(2)}) collective-permute-start(bf16[32,24,128]{2,1,0:T(8,128)(2,1)S(1)} %collective-permute-done.rest_0_), channel_id=1, source_target_pairs={{0,1},{1,0},{2,3},{3,2},{4,5},{5,4},{6,7},{7,6},{8,9},{9,8},{10,11... | collective-permute-start | bytes 589832 | tf_op jit(solution)/shard_map/ppermute | solution.py:40
  39.0 0.1 collective-permute-start.5
  39.1 0.4 collective-permute-start.6
  39.6 1.2 %shard_map.67.chosen_ref = bf16[6144,128]{1,0:T(8,128)(2,1)S(1)} custom-call(s32[270]{0:T(512)S(1)} %get-tuple-element.35.plan_ref, s32[1,256]{1,0:T(1,128)S(1)} %bitcast.1), custom_call_target="tpu_custom_call" | custom-call | flops 1620049920 | bytes 263680 | tf_op jit(solution)/shard_map/pallas_call | solution.py:458
  40.7 0.0 collective-permute-done.5.rest_2_
  40.7 0.0 collective-permute-done.6.rest_4_
  40.8 6.2 %shard_map.68 = (f32[3,1,6144]{2,1,0:T(1,128)S(1)}, f32[3,1,6144]{2,1,0:T(1,128)S(1)}, f32[3,1,6144]{2,1,0:T(1,128)S(1)}, f32[3,1,6144]{2,1,0:T(1,128)S(1)}, bf16[5,1024,128]{2,1,0:T(8,128)(2,1)S(1)}) custom-call(s32[270]{0:T(512)S(1)} %get-tuple-element.35.plan_ref, bf16[32,24,128]{2,1,0:T(8,128)(2,1)S(1)} %collective-permute-done.4.rest_0_, ...), custom_call_target="tpu_custom_call" | custom-call | flops 4860149760 | bytes 791040 | tf_op jit(solution)/shard_map/pallas_call | solution.py:469
  46.9 0.4 collective-permute-start.7
  47.3 0.5 collective-permute-start.8
  47.7 2.2 %collective-permute-start.9 = (f32[3,1,6144]{2,1,0:T(1,128)S(1)}, f32[3,1,6144]{2,1,0:T(1,128)S(1)}, u32[]{:S(2)}, u32[]{:S(2)}) collective-permute-start(f32[3,1,6144]{2,1,0:T(1,128)S(1)} %get-tuple-element.62), channel_id=1, source_target_pairs={{0,29},{1,30},{2,31},{3,0},{4,1},{5,2},{6,3},{7,4},{8,5},{9,6},{10... | collective-permute-start | bytes 221192 | tf_op jit(solution)/shard_map/ppermute | solution.py:48
  50.0 6.1 %shard_map.69.rest_2_ = f32[3,5,1,768]{3,2,1,0:T(1,128)S(1)} custom-call(s32[270]{0:T(512)S(1)} %get-tuple-element.35.plan_ref, bf16[5,1024,128]{2,1,0:T(8,128)(2,1)S(1)} %get-tuple-element.58.kept_ref, bf16[6,1030,128]{2,1,0:T(8,128)(2,1)S(1)} %copy-done.1, f32[3,1,6144]{2,1,0:T(1,128)S(1)} %get-tuple-element.59.before_ref), custom_call_target="tpu_custom_call" | custom-call | flops 4860149760 | bytes 791040 | tf_op jit(solution)/shard_map/pallas_call | solution.py:480
  56.1 0.0 collective-permute-done.7.rest_3_
  56.1 0.0 collective-permute-done.9.rest_5_
  56.1 1.5 %shard_map.70 = f32[3,256]{1,0:T(4,128)} custom-call(s32[270]{0:T(512)S(1)} %get-tuple-element.35.plan_ref, s32[1,256]{1,0:T(1,128)S(1)} %bitcast.2, bf16[6144,128]{1,0:T(8,128)(2,1)S(1)} %shard_map.67.chosen_ref, f32[3,2,1,768]{3,2,1,0:T(1,128)S(1)} %get-tuple-element.45.rest_6_.rest_0_, f32[3,1,1,768]{3,2,1,0:T(1,128)S(1)} %get-tuple-element.46.rest_10_.rest_1_, ...), custom_call_target="tpu_custom_call" | custom-call | tf_op jit(solution)/shard_map/pallas_call | solution.py:490
  (14 shorter events, 0.0 us)
Async XLA Ops:
  0.0 30.0 %copy-start.1 = (bf16[6,1030,128]{2,1,0:T(8,128)(2,1)S(1)}, bf16[6,1030,128]{2,1,0:T(8,128)(2,1)}, u32[]{:S(2)}) copy-start(bf16[6,1030,128]{2,1,0:T(8,128)(2,1)} %all_pages_ref.1) | copy-start | bytes 4746244
  0.0 30.0 %copy-start = (s32[256]{0:T(256)S(1)}, s32[256]{0:T(256)}, u32[]{:S(2)}) copy-start(s32[256]{0:T(256)} %len_hbm.1) | copy-start | bytes 3076
  0.0 30.0 %copy-start.4 = (s32[6]{0:T(128)S(1)}, s32[6]{0:T(128)}, u32[]{:S(2)}) copy-start(s32[6]{0:T(128)} %helper_hbm.1) | copy-start | bytes 76
  0.0 30.0 %copy-start.3 = (s32[3]{0:T(128)S(1)}, s32[3]{0:T(128)}, u32[]{:S(2)}) copy-start(s32[3]{0:T(128)} %offset_hbm.1) | copy-start | bytes 40
  0.0 30.0 %copy-start.2 = (s32[3]{0:T(128)S(1)}, s32[3]{0:T(128)}, u32[]{:S(2)}) copy-start(s32[3]{0:T(128)} %count_hbm.1) | copy-start | bytes 40
  23.0 7.1 %collective-permute-start.1 = (bf16[32,24,128]{2,1,0:T(8,128)(2,1)S(1)}, bf16[32,24,128]{2,1,0:T(8,128)(2,1)S(1)}, u32[]{:S(2)}, u32[]{:S(2)}) collective-permute-start(bf16[32,24,128]{2,1,0:T(8,128)(2,1)S(1)} %all_to_all.5.rest_0_), channel_id=1, source_target_pairs={{0,1},{1,0},{2,3},{3,2},{4,5},{5,4},{6,7},{7,6},{8,9},{9,8},{10,11... | collective-permute-start | bytes 589832 | tf_op jit(solution)/shard_map/ppermute | solution.py:40
  25.8 9.6 %collective-permute-start = (bf16[32,24,128]{2,1,0:T(8,128)(2,1)S(1)}, bf16[32,24,128]{2,1,0:T(8,128)(2,1)S(1)}, u32[]{:S(2)}, u32[]{:S(2)}) collective-permute-start(bf16[32,24,128]{2,1,0:T(8,128)(2,1)S(1)} %all_to_all.5.rest_0_), channel_id=1, source_target_pairs={{0,128},{1,129},{2,130},{3,131},{4,132},{5,133},{6,134},{7,135},{8... | collective-permute-start | bytes 589832 | tf_op jit(solution)/shard_map/ppermute | solution.py:35
  28.6 9.6 %collective-permute-start.3 = (bf16[32,24,128]{2,1,0:T(8,128)(2,1)S(1)}, bf16[32,24,128]{2,1,0:T(8,128)(2,1)S(1)}, u32[]{:S(2)}, u32[]{:S(2)}) collective-permute-start(bf16[32,24,128]{2,1,0:T(8,128)(2,1)S(1)} %all_to_all.5.rest_0_), channel_id=1, source_target_pairs={{0,144},{1,145},{2,146},{3,147},{4,148},{5,149},{6,150},{7,151},{8... | collective-permute-start | bytes 589832 | tf_op jit(solution)/shard_map/ppermute | solution.py:35
  29.4 8.8 %collective-permute-start.2 = (bf16[32,24,128]{2,1,0:T(8,128)(2,1)S(1)}, bf16[32,24,128]{2,1,0:T(8,128)(2,1)S(1)}, u32[]{:S(2)}, u32[]{:S(2)}) collective-permute-start(bf16[32,24,128]{2,1,0:T(8,128)(2,1)S(1)} %all_to_all.5.rest_0_), channel_id=1, source_target_pairs={{0,16},{1,17},{2,18},{3,19},{4,20},{5,21},{6,22},{7,23},{8,24},{9,... | collective-permute-start | bytes 589832 | tf_op jit(solution)/shard_map/ppermute | solution.py:35
  38.2 2.5 %collective-permute-start.4 = (bf16[32,24,128]{2,1,0:T(8,128)(2,1)S(1)}, bf16[32,24,128]{2,1,0:T(8,128)(2,1)S(1)}, u32[]{:S(2)}, u32[]{:S(2)}) collective-permute-start(bf16[32,24,128]{2,1,0:T(8,128)(2,1)S(1)} %collective-permute-done.rest_0_), channel_id=1, source_target_pairs={{0,1},{1,0},{2,3},{3,2},{4,5},{5,4},{6,7},{7,6},{8,9},{9,8},{10,11... | collective-permute-start | bytes 589832 | tf_op jit(solution)/shard_map/ppermute | solution.py:40
  39.0 1.7 %collective-permute-start.5 = (bf16[32,24,128]{2,1,0:T(8,128)(2,1)S(1)}, bf16[32,24,128]{2,1,0:T(8,128)(2,1)S(1)}, u32[]{:S(2)}, u32[]{:S(2)}) collective-permute-start(bf16[32,24,128]{2,1,0:T(8,128)(2,1)S(1)} %collective-permute-done.2.rest_1_), channel_id=1, source_target_pairs={{0,1},{1,0},{2,3},{3,2},{4,5},{5,4},{6,7},{7,6},{8,9},{9,8},{10,11... | collective-permute-start | bytes 589832 | tf_op jit(solution)/shard_map/ppermute | solution.py:40
  39.1 1.6 %collective-permute-start.6 = (bf16[32,24,128]{2,1,0:T(8,128)(2,1)S(1)}, bf16[32,24,128]{2,1,0:T(8,128)(2,1)S(1)}, u32[]{:S(2)}, u32[]{:S(2)}) collective-permute-start(bf16[32,24,128]{2,1,0:T(8,128)(2,1)S(1)} %collective-permute-done.3.rest_3_), channel_id=1, source_target_pairs={{0,1},{1,0},{2,3},{3,2},{4,5},{5,4},{6,7},{7,6},{8,9},{9,8},{10,11... | collective-permute-start | bytes 589832 | tf_op jit(solution)/shard_map/ppermute | solution.py:40
  46.9 9.2 %collective-permute-start.7 = (f32[3,1,6144]{2,1,0:T(1,128)S(1)}, f32[3,1,6144]{2,1,0:T(1,128)S(1)}, u32[]{:S(2)}, u32[]{:S(2)}) collective-permute-start(f32[3,1,6144]{2,1,0:T(1,128)S(1)} %get-tuple-element.60), channel_id=1, source_target_pairs={{0,31},{1,0},{2,1},{3,2},{4,3},{5,4},{6,5},{7,6},{8,7},{9,8},{10,9... | collective-permute-start | bytes 221192 | tf_op jit(solution)/shard_map/ppermute | solution.py:48
  47.3 8.8 %collective-permute-start.8 = (f32[3,1,6144]{2,1,0:T(1,128)S(1)}, f32[3,1,6144]{2,1,0:T(1,128)S(1)}, u32[]{:S(2)}, u32[]{:S(2)}) collective-permute-start(f32[3,1,6144]{2,1,0:T(1,128)S(1)} %get-tuple-element.61), channel_id=1, source_target_pairs={{0,30},{1,31},{2,0},{3,1},{4,2},{5,3},{6,4},{7,5},{8,6},{9,7},{10,... | collective-permute-start | bytes 221192 | tf_op jit(solution)/shard_map/ppermute | solution.py:48
  47.7 8.4 %collective-permute-start.9 = (f32[3,1,6144]{2,1,0:T(1,128)S(1)}, f32[3,1,6144]{2,1,0:T(1,128)S(1)}, u32[]{:S(2)}, u32[]{:S(2)}) collective-permute-start(f32[3,1,6144]{2,1,0:T(1,128)S(1)} %get-tuple-element.62), channel_id=1, source_target_pairs={{0,29},{1,30},{2,31},{3,0},{4,1},{5,2},{6,3},{7,4},{8,5},{9,6},{10... | collective-permute-start | bytes 221192 | tf_op jit(solution)/shard_map/ppermute | solution.py:48

commit v3 on v2

--- a/solution.py
+++ b/solution.py
@@ -13,6 +13,7 @@
 NX, NY, NZ, NC = 4, 4, 8, 2
 CHUNK = NY * NZ
 TILE = 256
+WIDE = 2 * TILE
 lowest = -1e30
 VMEM_LIMIT = 48 * 1024 * 1024
 TRANSPOSED = (((1,), (1,)), ((), ()))
@@ -124,56 +125,75 @@
 def over_tiles(total, visit):
     tiles = (total + TILE - 1) // TILE
 
-    def double(i, _):
-        visit(pl.multiple_of(i * (2 * TILE), 2 * TILE), 2 * TILE)
+    def four(i, _):
+        visit(pl.multiple_of(i * (4 * TILE), 4 * TILE), 4 * TILE)
         return 0
 
-    lax.fori_loop(0, tiles // 2, double, 0)
+    lax.fori_loop(0, tiles // 4, four, 0)
+    done = tiles // 4 * 4
+
+    @pl.when(tiles % 4 >= 2)
+    def _():
+        visit(pl.multiple_of(done * TILE, 4 * TILE), 2 * TILE)
 
     @pl.when(tiles % 2 == 1)
     def _():
         visit(pl.multiple_of((tiles - 1) * TILE, TILE), TILE)
 
 
+def from_column(table_ref, first, span):
+    if isinstance(first, int):
+        return table_ref[:, first : first + span]
+    lanes = 128
+    base = pl.multiple_of(first // lanes * lanes, lanes)
+    window = table_ref[:, pl.ds(base, span + lanes)]
+    return pltpu.roll(window, lax.rem(span + lanes - (first - base), span + lanes), 1)[:, :span]
+
+
 def own_position():
     return lax.axis_index("xh") * 2 + lax.axis_index("xl"), lax.axis_index("c")
 
 
-def all_slots(live_ref, base, at, size, ids, pages_ref, tails, slot_ref, outs, write):
-    token_rows = live_ref[pl.ds(base + at, size), :].astype(jnp.bfloat16)
-    slot_ref[...] = jnp.full(slot_ref.shape, lowest, jnp.float32)
-    for slot, best in zip(ids, page_best(token_rows, pages_ref, tails)):
-        slot_ref[slot, :, :size] = jnp.maximum(slot_ref[slot, :, :size], best)
-    docs = outs[0].shape[0]
-    for distance in range(SPILL + 1):
-        for j in range(docs):
-            write(outs[distance], j, slot_ref[distance * docs + j, :, :size])
-    return token_rows
-
-
-def whole_chunks(specs, plan_ref, sources, outs, pages_ref, live_ref, slot_ref, ids, tails):
+def over_chunks(count, total_of, span, visit):
+    def each(i, _):
+        def tile(k, _):
+            visit(i, pl.multiple_of(jnp.minimum(k * WIDE, span - WIDE), TILE))
+            return 0
+
+        lax.fori_loop(0, (total_of(i) + WIDE - 1) // WIDE, tile, 0)
+        return 0
+
+    lax.fori_loop(0, count, each, 0)
+
+
+def whole_chunks(specs, plan_ref, sources, outs, pages_ref, live_ref, slot_ref, note_ref, ids, tails):
     x, c = own_position()
     room = live_ref.shape[0] // len(specs)
-    totals = [
-        compact(plan_ref, live_ref, i * room, chunk_of(spec, x, c), source)
-        for i, (spec, source) in enumerate(zip(specs, sources))
-    ]
-    for i in range(len(specs)):
-
-        def visit(at, size, i=i):
-            def write(out, j, value):
-                out[j, i, :, pl.ds(at, size)] = value
-
-            all_slots(live_ref, i * room, at, size, ids, pages_ref, tails, slot_ref, outs, write)
-
-        over_tiles(totals[i], visit)
+    for i, (spec, source) in enumerate(zip(specs, sources)):
+        note_ref[i] = compact(plan_ref, live_ref, i * room, chunk_of(spec, x, c), source)
+
+    docs, span = outs[0].shape[1:]
+
+    def visit(i, at):
+        base = pl.multiple_of(i * room, TILE)
+        token_rows = live_ref[pl.ds(base + at, WIDE), :].astype(jnp.bfloat16)
+        slot_ref[...] = jnp.full(slot_ref.shape, lowest, jnp.float32)
+        for slot, best in zip(ids, page_best(token_rows, pages_ref, tails)):
+            row = pl.ds(slot, 1)
+            slot_ref[row, :] = jnp.maximum(slot_ref[row, :], best)
+        for distance in range(SPILL + 1):
+            outs[distance][i, :, pl.ds(at, WIDE)] = slot_ref[
+                distance * docs : (distance + 1) * docs, :
+            ]
+
+    over_chunks(len(specs), lambda i: note_ref[i], span, visit)
 
 
 def first_kernel(specs, len_hbm, count_hbm, offset_hbm, helper_hbm, *rest):
     sources, rest = rest[: len(specs)], rest[len(specs) :]
     pages_ref, rest = rest[0], rest[1:]
     outs, rest = rest[: SPILL + 1], rest[SPILL + 1 :]
-    plan_ref, count_ref, offset_ref, helper_ref, live_ref, tail_ref, slot_ref, sem = rest
+    plan_ref, count_ref, offset_ref, helper_ref, live_ref, tail_ref, slot_ref, note_ref, sem = rest
     pages = pages_ref.shape[0]
     moves = [
         pltpu.make_async_copy(source, target, sem.at[i])
@@ -197,17 +217,17 @@
         plan_ref[at + k] = ids[k]
     for chunk in range(NX * NC):
         plan_ref[at + pages + chunk] = chunk_total(plan_ref, chunk // NC, chunk % NC)
-    whole_chunks(specs, plan_ref, sources, outs, pages_ref, live_ref, slot_ref, ids, tails)
+    whole_chunks(specs, plan_ref, sources, outs, pages_ref, live_ref, slot_ref, note_ref, ids, tails)
 
 
 def more_kernel(specs, queries, plan_ref, *rest):
     sources, rest = rest[: len(specs)], rest[len(specs) :]
     pages_ref, rest = rest[0], rest[1:]
     outs, rest = rest[: SPILL + 1], rest[SPILL + 1 :]
-    live_ref, tail_ref, slot_ref = rest
+    live_ref, tail_ref, slot_ref, note_ref = rest
     ids = [plan_ref[queries + k] for k in range(pages_ref.shape[0])]
     tails = fill_tails(pages_ref, tail_ref)
-    whole_chunks(specs, plan_ref, sources, outs, pages_ref, live_ref, slot_ref, ids, tails)
+    whole_chunks(specs, plan_ref, sources, outs, pages_ref, live_ref, slot_ref, note_ref, ids, tails)
 
 
 def chunk_count(plan_ref, chunk):
@@ -260,18 +280,17 @@
     return starts, starts + lens
 
 
-def late_kernel(specs, placed, queries, plan_ref, *rest):
+def late_kernel(specs, placed, queries, plan_ref, nothing_ref, *rest):
     sources, rest = rest[: len(specs)], rest[len(specs) :]
     all_pages_ref, rest = rest[0], rest[1:]
     before, rest = rest[: len(placed) * (SPILL + 1)], rest[len(placed) * (SPILL + 1) :]
     outs, rest = rest[: SPILL + 1], rest[SPILL + 1 :]
-    kept_ref, live_ref, tail_ref, slot_ref = rest
-    docs = outs[0].shape[0]
+    kept_ref, live_ref, tail_ref, table_ref = rest
+    docs, columns_all = outs[0].shape
     pages = all_pages_ref.shape[0]
     pages_ref = all_pages_ref.at[pl.ds(docs, pages - docs)]
     x, c = own_position()
-    room = kept_ref.shape[1]
-    span = outs[0].shape[2] // (NX * NC)
+    span = columns_all // (NX * NC)
 
     def column(spec):
         chunk = chunk_of(spec, x, c)
@@ -280,59 +299,67 @@
     for group, group_specs in enumerate(placed):
         for i, spec in enumerate(group_specs):
             for distance in range(SPILL + 1):
-                for j in range(docs):
-                    outs[distance][j, :, pl.ds(column(spec), span)] = before[
-                        group * (SPILL + 1) + distance
-                    ][j, i]
+                outs[distance][:, pl.ds(column(spec), span)] = before[
+                    group * (SPILL + 1) + distance
+                ][i]
     ids = [plan_ref[queries + k] for k in range(docs, pages)]
     tails = fill_tails(pages_ref, tail_ref)
-    totals = [
-        compact(plan_ref, live_ref, i * room, chunk_of(spec, x, c), source)
-        for i, (spec, source) in enumerate(zip(specs, sources))
-    ]
-    for i, spec in enumerate(specs):
-        where = column(spec)
-
-        def visit(at, size, i=i, where=where):
-            to = pl.multiple_of(where + at, TILE)
-
-            def write(out, j, value):
-                out[j, :, pl.ds(to, size)] = value
-
-            kept_ref[i, pl.ds(at, size), :] = all_slots(
-                live_ref, i * room, at, size, ids, pages_ref, tails, slot_ref, outs, write
-            )
-
-        over_tiles(totals[i], visit)
-
-
-def home_kernel(specs, queries, plan_ref, kept_ref, all_pages_ref, before_ref, out_ref, tail_ref):
-    docs, _, _, span = out_ref.shape
+    firsts = [0]
+    for spec, source in zip(specs, sources):
+        chunk = chunk_of(spec, x, c)
+        compact(plan_ref, live_ref, firsts[-1], chunk, source)
+        firsts.append(firsts[-1] + chunk_count(plan_ref, chunk))
+
+    nothing = nothing_ref[0:1, 0:1]
+
+    def visit(at, size):
+        token_rows = live_ref[pl.ds(at, size), :].astype(jnp.bfloat16)
+        kept_ref[pl.ds(at, size), :] = token_rows
+        here = pl.ds(at, size)
+        table_ref[:, here] = jnp.broadcast_to(nothing, (table_ref.shape[0], size))
+        for slot, best in zip(ids, page_best(token_rows, pages_ref, tails)):
+            row = pl.ds(slot, 1)
+            table_ref[row, here] = jnp.maximum(table_ref[row, here], best)
+
+    over_tiles(firsts[-1], visit)
+    for spec, first in zip(specs, firsts):
+        value = from_column(table_ref, first, span)
+        to = column(spec)
+        for distance in range(SPILL + 1):
+            outs[distance][:, pl.ds(to, span)] = value[distance * docs : (distance + 1) * docs]
+
+
+def home_kernel(
+    specs, queries, plan_ref, kept_ref, all_pages_ref, before_ref, out_ref, tail_ref, table_ref
+):
+    docs, span = out_ref.shape[1:]
     pages_ref = all_pages_ref.at[pl.ds(0, docs)]
     x, c = own_position()
     ids = [plan_ref[queries + k] for k in range(docs)]
     tails = fill_tails(pages_ref, tail_ref)
-    for i, spec in enumerate(specs):
-        chunk = chunk_of(spec, x, c)
-        where = pl.multiple_of((chunk[0] * NC + chunk[1]) * span, TILE)
-
-        def visit(at, size, i=i, where=where):
-            to = pl.multiple_of(where + at, TILE)
-            rows = page_best(kept_ref[i, pl.ds(at, size), :], pages_ref, tails)
-            for j in range(docs):
-                out_ref[j, i, :, pl.ds(at, size)] = before_ref[j, :, pl.ds(to, size)]
-            for slot, best in zip(ids, rows):
-                out_ref[slot, i, :, pl.ds(at, size)] = jnp.maximum(
-                    out_ref[slot, i, :, pl.ds(at, size)], best
-                )
-
-        over_tiles(chunk_count(plan_ref, chunk), visit)
+    chunks = [chunk_of(spec, x, c) for spec in specs]
+    firsts = [0]
+    for chunk in chunks:
+        firsts.append(firsts[-1] + chunk_count(plan_ref, chunk))
+
+    def visit(at, size):
+        here = pl.ds(at, size)
+        table_ref[:, here] = jnp.full((table_ref.shape[0], size), lowest, jnp.float32)
+        for slot, best in zip(ids, page_best(kept_ref[here, :], pages_ref, tails)):
+            row = pl.ds(slot, 1)
+            table_ref[row, here] = jnp.maximum(table_ref[row, here], best)
+
+    over_tiles(firsts[-1], visit)
+    for i, (chunk, first) in enumerate(zip(chunks, firsts)):
+        value = from_column(table_ref, first, span)
+        to = pl.multiple_of((chunk[0] * NC + chunk[1]) * span, TILE)
+        out_ref[i] = jnp.maximum(before_ref[:, pl.ds(to, span)], value[:docs])
 
 
 def scores_kernel(groups, plan_ref, lens_ref, chosen_ref, *rest):
     homes, rest = rest[: len(groups)], rest[len(groups) :]
     received, (out_ref, acc_ref) = rest[:SPILL], rest[SPILL:]
-    docs, _, columns_all = received[0].shape
+    docs, columns_all = received[0].shape
     lens = lens_ref[...]
     span = columns_all // (NX * NC)
     x, c = own_position()
@@ -344,35 +371,46 @@
     ]
 
     def visit(at, size):
+        added = []
         for home_ref, i, chunk in parts_list:
             to = pl.multiple_of((chunk[0] * NC + chunk[1]) * span + at, TILE)
-            total = chunk_count(plan_ref, chunk)
-            live = lax.broadcasted_iota(jnp.int32, (1, size), 1) + at < total
-            parts = []
-            for j in range(docs):
-                value = home_ref[j, i, :, pl.ds(at, size)]
-                for ref in received:
-                    value = jnp.maximum(value, ref[j, :, pl.ds(to, size)])
-                value = jnp.where(live, value, 0.0)
-                high = value.astype(jnp.bfloat16).astype(jnp.float32)
-                left = value - high
-                middle = left.astype(jnp.bfloat16).astype(jnp.float32)
-                parts += [high, middle, left - middle]
-            parts.append(jnp.zeros((acc_ref.shape[1] - len(parts), size), jnp.float32))
-            left_side = jnp.concatenate(parts, axis=0).astype(jnp.bfloat16)
-            x_hi = chunk[0] // 2
-            acc_ref[x_hi] = acc_ref[x_hi] + jnp.dot(
-                left_side, chosen_ref[pl.ds(to, size), :], preferred_element_type=jnp.float32
+            live = lax.broadcasted_iota(jnp.int32, (docs, size), 1) + at < chunk_count(
+                plan_ref, chunk
             )
-
-    over_tiles(most_tokens(plan_ref), visit)
+            value = home_ref[i, :, pl.ds(at, size)]
+            for ref in received:
+                value = jnp.maximum(value, ref[:, pl.ds(to, size)])
+            value = jnp.where(live, value, 0.0)
+            value = jnp.concatenate([value, jnp.zeros((8 - docs, size), jnp.float32)], axis=0)
+            high = value.astype(jnp.bfloat16).astype(jnp.float32)
+            left = value - high
+            middle = left.astype(jnp.bfloat16).astype(jnp.float32)
+            pieces = [high, middle, left - middle, jnp.zeros((8, size), jnp.float32)]
+            left_side = jnp.concatenate(pieces, axis=0).astype(jnp.bfloat16)
+            added.append(
+                jnp.dot(
+                    left_side, chosen_ref[pl.ds(to, size), :], preferred_element_type=jnp.float32
+                )
+            )
+        for (_, _, chunk), value in zip(parts_list, added):
+            acc_ref[chunk[0] // 2] = acc_ref[chunk[0] // 2] + value
+
+    tiles = (most_tokens(plan_ref) + TILE - 1) // TILE
+
+    @pl.when(tiles >= 2)
+    def _():
+        visit(0, 2 * TILE)
+
+    @pl.when(tiles % 2 == 1)
+    def _():
+        visit(pl.multiple_of((tiles - 1) * TILE, TILE), TILE)
+
     half = acc_ref.shape[2]
     for x_hi in range(acc_ref.shape[0]):
         lanes = slice(x_hi * half, (x_hi + 1) * half)
         divisor = lens[:, lanes].astype(jnp.float32)
-        for j in range(docs):
-            high, middle, low = (acc_ref[x_hi, 3 * j + i : 3 * j + i + 1, :] for i in range(3))
-            out_ref[j : j + 1, lanes] = ((high + middle) + low) / divisor
+        high, middle, low = (acc_ref[x_hi, 8 * i : 8 * i + docs, :] for i in range(3))
+        out_ref[:, lanes] = ((high + middle) + low) / divisor
 
 
 SMEM = pl.BlockSpec(memory_space=pltpu.SMEM)
@@ -380,9 +418,8 @@
 HBM = pl.BlockSpec(memory_space=pltpu.HBM)
 
 
-def copies_kernel(block_ref, out_ref):
-    for i in range(out_ref.shape[0]):
-        out_ref[i] = block_ref[0]
+def lowest_kernel(out_ref):
+    out_ref[...] = jnp.full(out_ref.shape, lowest, jnp.float32)
 
 
 def local(queries, query_len, pages, page_count, page_offset, helper_doc):
@@ -393,13 +430,15 @@
     span = columns // (NX * NC)
     room = span + TILE
     params = pltpu.CompilerParams(vmem_limit_bytes=VMEM_LIMIT)
-    whole = [jax.ShapeDtypeStruct((docs, 1, columns), jnp.float32)] * (SPILL + 1)
-    slots = pltpu.VMEM(((SPILL + 1) * docs, 1, 2 * TILE), jnp.float32)
+    whole = [jax.ShapeDtypeStruct((docs, columns), jnp.float32)] * (SPILL + 1)
+    slots = pltpu.VMEM((16, WIDE), jnp.float32)
+    notes = pltpu.SMEM((16,), jnp.int32)
     row = query_len[None, :]
     own, far, rest = [(0, 0), (0, 1)], [(2, 0)], [(2, 1), (1, 0), (1, 1), (3, 0), (3, 1)]
+    pool = len(rest) * span + 2 * WIDE
 
     def part(specs):
-        return [jax.ShapeDtypeStruct((docs, len(specs), 1, span), jnp.float32)] * (SPILL + 1)
+        return [jax.ShapeDtypeStruct((len(specs), docs, span), jnp.float32)] * (SPILL + 1)
 
     def tail_room(count):
         return pltpu.VMEM((8 * count + 8 * count % 16, width), jnp.float32)
@@ -412,13 +451,14 @@
             flops=2 * rows * columns * width, bytes_accessed=rows * width * 2, transcendentals=0
         )
 
-    copies = pl.pallas_call(
-        copies_kernel,
-        out_shape=jax.ShapeDtypeStruct((CHUNK, tokens, width), jnp.bfloat16),
-        in_specs=[VMEM],
+    nothing = pl.pallas_call(
+        lowest_kernel,
+        out_shape=jax.ShapeDtypeStruct((8, 128), jnp.float32),
         out_specs=VMEM,
         cost_estimate=cost(pages.shape[0] * pages.shape[1]),
-    )(queries)
+    )()
+    queries, nothing = lax.optimization_barrier((queries, nothing))
+    copies = jnp.broadcast_to(queries, (CHUNK, tokens, width))
     mine = lax.all_to_all(copies, ("y", "z"), 0, 0, tiled=True)
     mine_other = other_core(mine)
     two, one, three = [along_x(mine, steps) for steps in (2, 1, 3)]
@@ -436,6 +476,7 @@
             live_room(own),
             tail_room(pages.shape[0]),
             slots,
+            notes,
             pltpu.SemaphoreType.DMA((4,)),
         ],
         compiler_params=params,
@@ -448,7 +489,7 @@
         out_shape=part(far),
         in_specs=[SMEM] + [VMEM] * (len(far) + 1),
         out_specs=[VMEM] * (SPILL + 1),
-        scratch_shapes=[live_room(far), tail_room(pages.shape[0]), slots],
+        scratch_shapes=[live_room(far), tail_room(pages.shape[0]), slots, notes],
         compiler_params=params,
         cost_estimate=cost(700),
     )(plan, two, pages)
@@ -468,13 +509,17 @@
 
     *partials, kept = pl.pallas_call(
         functools.partial(late_kernel, rest, (own, far), total),
-        out_shape=whole + [jax.ShapeDtypeStruct((len(rest), room, width), jnp.bfloat16)],
-        in_specs=[SMEM] + [VMEM] * (len(rest) + 1 + 2 * (SPILL + 1)),
+        out_shape=whole + [jax.ShapeDtypeStruct((pool, width), jnp.bfloat16)],
+        in_specs=[SMEM] + [VMEM] * (len(rest) + 2 + 2 * (SPILL + 1)),
         out_specs=[VMEM] * (SPILL + 2),
-        scratch_shapes=[live_room(rest), tail_room(pages.shape[0] - docs), slots],
+        scratch_shapes=[
+            pltpu.VMEM((pool, width), jnp.float32),
+            tail_room(pages.shape[0] - docs),
+            pltpu.VMEM((16, pool), jnp.float32),
+        ],
         compiler_params=params,
         cost_estimate=cost((pages.shape[0] - docs) * pages.shape[1]),
-    )(plan, *arrived, pages, *own_out, *far_out)
+    )(plan, nothing, *arrived, pages, *own_out, *far_out)
     received = [along_blk(partials[distance], -distance) for distance in range(1, SPILL + 1)]
 
     rest_home = pl.pallas_call(
@@ -482,7 +527,7 @@
         out_shape=part(rest)[0],
         in_specs=[SMEM] + [VMEM] * 3,
         out_specs=VMEM,
-        scratch_shapes=[tail_room(docs)],
+        scratch_shapes=[tail_room(docs), pltpu.VMEM((8, pool), jnp.float32)],
         compiler_params=params,
         cost_estimate=cost(docs * pages.shape[1]),
     )(plan, kept, pages, partials[0])
@@ -492,7 +537,7 @@
         out_shape=jax.ShapeDtypeStruct((docs, total), jnp.float32),
         in_specs=[SMEM] + [VMEM] * (SPILL + 5),
         out_specs=VMEM,
-        scratch_shapes=[pltpu.VMEM((2, 16, total // 2), jnp.float32)],
+        scratch_shapes=[pltpu.VMEM((2, 32, total // 2), jnp.float32)],
         compiler_params=params,
     )(plan, row, chosen, own_out[0], far_out[0], rest_home, *received)
 

time: 57.9 us -> 56.3 us (0.972)
  Pallas kernels: 24.3 us -> 20.6 us
  waiting for transfers between devices: 0.33 us -> 2.67 us
    ppermute x3, waiting for transfers between devices: 0.01 us -> 2.36 us  [along_blk(): return lax.ppermute(value, AXES, pairs)]
    pallas_call x1, Pallas kernels: 6.13 us -> 4.53 us  [local(): pl.pallas_call(functools.partial(home_kernel, rest, total), out_shape=par...]
    pallas_call x1, Pallas kernels: 6.15 us -> 4.98 us  [local(): pl.pallas_call(functools.partial(late_kernel, rest, (own, far), total), o...]
    pallas_call x1, Pallas kernels: 1.5 us -> 0.6 us  [local(): pl.pallas_call(lowest_kernel, out_shape=jax.ShapeDtypeStruct((8, 128), jn...]
  transfers between devices with their start and end apart: 10 -> 10, of which waited for: 1 -> 2; matrix products, arithmetic and copies ran while one was open for 0% -> 0% of each run, Pallas kernels for 26% -> 24%
where the time goes in v3:
time: 56.3 us; the launch traced here: 56.2 us
  blocking collectives  21.2 us (38%)
  Pallas kernels  20.6 us (37%)
  starting transfers between devices  11.4 us (20%)
  waiting for transfers between devices  2.67 us (5%)
    all_to_all x1, blocking collectives, local(): mine = lax.all_to_all(copies, ('y', 'z'), 0, 0, tiled=True)  21.2 us
    pallas_call x1, Pallas kernels, local(): pl.pallas_call(functools.partial(first_kernel, own), out_shape=part(own)...  5.32 us
    pallas_call x1, Pallas kernels, local(): pl.pallas_call(functools.partial(late_kernel, rest, (own, far), total), o...  4.98 us
    pallas_call x1, Pallas kernels, local(): pl.pallas_call(functools.partial(home_kernel, rest, total), out_shape=par...  4.53 us
    ppermute x3, starting transfers between devices, along_x(): return lax.ppermute(value, AXES, pairs)  4.21 us
    ppermute x4, starting transfers between devices, other_core(): return lax.ppermute(value, AXES, pairs)  4.14 us
    ppermute x3, starting transfers between devices, along_blk(): return lax.ppermute(value, AXES, pairs)  3.08 us
    pallas_call x1, Pallas kernels, local(): pl.pallas_call(functools.partial(more_kernel, far, total), out_shape=part...  2.5 us
  transfers between devices with their start and end apart: 10, of which 2 were waited for; matrix products, arithmetic and copies ran while one was open for 0% of the time, Pallas kernels for 24%

profile of v3, /device:TPU:1, one launch (start us, length us, event | category | flops | bytes accessed | tf_op | source)
XLA Modules:
  0.0 56.2 jit_solution(5489531895602170281)
XLA Ops:
  0.0 0.6 %shard_map.64.nothing_ref = f32[8,128]{1,0:T(8,128)} custom-call(), custom_call_target="tpu_custom_call" | custom-call | flops 9720299520 | bytes 1582080 | tf_op jit(solution)/shard_map/pallas_call | solution.py:454
  0.6 0.1 copy-done.6
  0.7 21.2 %all_to_all.5.rest_0_ = bf16[32,24,128]{2,1,0:T(8,128)(2,1)S(1)} all-to-all(bf16[32,24,128]{2,1,0:T(8,128)(2,1)S(1)} %broadcast_in_dim.11), channel_id=1, replica_groups=mesh['xh'=2,'y'=4,'xl'=2,'z'=8,'c'=2] {'y','z'}, dimensions={0} | all-to-all | bytes 393216 | tf_op jit(solution)/shard_map/all_to_all | solution.py:462
  22.0 2.8 %collective-permute-start.1 = (bf16[32,24,128]{2,1,0:T(8,128)(2,1)S(1)}, bf16[32,24,128]{2,1,0:T(8,128)(2,1)S(1)}, u32[]{:S(2)}, u32[]{:S(2)}) collective-permute-start(bf16[32,24,128]{2,1,0:T(8,128)(2,1)S(1)} %all_to_all.5.rest_0_), channel_id=1, source_target_pairs={{0,1},{1,0},{2,3},{3,2},{4,5},{5,4},{6,7},{7,6},{8,9},{9,8},{10,11... | collective-permute-start | bytes 589832 | tf_op jit(solution)/shard_map/ppermute | solution.py:41
  24.8 2.7 %collective-permute-start = (bf16[32,24,128]{2,1,0:T(8,128)(2,1)S(1)}, bf16[32,24,128]{2,1,0:T(8,128)(2,1)S(1)}, u32[]{:S(2)}, u32[]{:S(2)}) collective-permute-start(bf16[32,24,128]{2,1,0:T(8,128)(2,1)S(1)} %all_to_all.5.rest_0_), channel_id=1, source_target_pairs={{0,128},{1,129},{2,130},{3,131},{4,132},{5,133},{6,134},{7,135},{8... | collective-permute-start | bytes 589832 | tf_op jit(solution)/shard_map/ppermute | solution.py:36
  27.6 0.9 %collective-permute-start.3 = (bf16[32,24,128]{2,1,0:T(8,128)(2,1)S(1)}, bf16[32,24,128]{2,1,0:T(8,128)(2,1)S(1)}, u32[]{:S(2)}, u32[]{:S(2)}) collective-permute-start(bf16[32,24,128]{2,1,0:T(8,128)(2,1)S(1)} %all_to_all.5.rest_0_), channel_id=1, source_target_pairs={{0,144},{1,145},{2,146},{3,147},{4,148},{5,149},{6,150},{7,151},{8... | collective-permute-start | bytes 589832 | tf_op jit(solution)/shard_map/ppermute | solution.py:36
  28.4 0.6 %collective-permute-start.2 = (bf16[32,24,128]{2,1,0:T(8,128)(2,1)S(1)}, bf16[32,24,128]{2,1,0:T(8,128)(2,1)S(1)}, u32[]{:S(2)}, u32[]{:S(2)}) collective-permute-start(bf16[32,24,128]{2,1,0:T(8,128)(2,1)S(1)} %all_to_all.5.rest_0_), channel_id=1, source_target_pairs={{0,16},{1,17},{2,18},{3,19},{4,20},{5,21},{6,22},{7,23},{8,24},{9,... | collective-permute-start | bytes 589832 | tf_op jit(solution)/shard_map/ppermute | solution.py:36
  29.0 0.0 collective-permute-done.1.rest_1_
  29.1 5.3 %shard_map.65 = (f32[2,3,768]{2,1,0:T(4,128)S(1)}, f32[2,3,768]{2,1,0:T(4,128)S(1)}, f32[2,3,768]{2,1,0:T(4,128)S(1)}, f32[2,3,768]{2,1,0:T(4,128)S(1)}, s32[270]{0:T(512)S(1)}) custom-call(s32[256]{0:T(256)S(1)} %copy-done, s32[3]{0:T(128)S(1)} %copy-done.2, s32[3]{0:T(128)S(1)} %copy-done.3, s32[6]{0:T(128)S(1)} %copy-done.4, ...), custom_call_target="tpu_custom_call" | custom-call | flops 1101004800 | bytes 179200 | tf_op jit(solution)/shard_map/pallas_call | solution.py:466
  34.4 2.5 %shard_map.66 = (f32[1,3,768]{2,1,0:T(4,128)S(1)}, f32[1,3,768]{2,1,0:T(4,128)S(1)}, f32[1,3,768]{2,1,0:T(4,128)S(1)}, f32[1,3,768]{2,1,0:T(4,128)S(1)}) custom-call(s32[270]{0:T(512)S(1)} %get-tuple-element.38.plan_ref, bf16[32,24,128]{2,1,0:T(8,128)(2,1)S(1)} %collective-permute-done.rest_0_, bf16[6,1030,128]{2,1,0:T(8,128)(2,1)S(1)} %copy-done.1), custom_call_target="tpu_custom_call" | custom-call | flops 1101004800 | bytes 179200 | tf_op jit(solution)/shard_map/pallas_call | solution.py:487
  36.9 0.3 collective-permute-done.3.rest_3_
  37.2 0.0 collective-permute-done.2.rest_1_
  37.2 0.8 %collective-permute-start.4 = (bf16[32,24,128]{2,1,0:T(8,128)(2,1)S(1)}, bf16[32,24,128]{2,1,0:T(8,128)(2,1)S(1)}, u32[]{:S(2)}, u32[]{:S(2)}) collective-permute-start(bf16[32,24,128]{2,1,0:T(8,128)(2,1)S(1)} %collective-permute-done.rest_0_), channel_id=1, source_target_pairs={{0,1},{1,0},{2,3},{3,2},{4,5},{5,4},{6,7},{7,6},{8,9},{9,8},{10,11... | collective-permute-start | bytes 589832 | tf_op jit(solution)/shard_map/ppermute | solution.py:41
  38.0 0.0 collective-permute-start.5
  38.0 0.5 collective-permute-start.6
  38.5 1.2 %shard_map.67.chosen_ref = bf16[6144,128]{1,0:T(8,128)(2,1)S(1)} custom-call(s32[270]{0:T(512)S(1)} %get-tuple-element.38.plan_ref, s32[1,256]{1,0:T(1,128)S(1)} %bitcast.2), custom_call_target="tpu_custom_call" | custom-call | flops 1620049920 | bytes 263680 | tf_op jit(solution)/shard_map/pallas_call | solution.py:499
  39.7 0.0 collective-permute-done.6.rest_4_
  39.7 5.0 %shard_map.68 = (f32[3,6144]{1,0:T(4,128)S(1)}, f32[3,6144]{1,0:T(4,128)S(1)}, f32[3,6144]{1,0:T(4,128)S(1)}, f32[3,6144]{1,0:T(4,128)S(1)}, bf16[4864,128]{1,0:T(8,128)(2,1)S(1)}) custom-call(s32[270]{0:T(512)S(1)} %get-tuple-element.38.plan_ref, f32[8,128]{1,0:T(8,128)S(1)} %copy-done.5, bf16[32,24,128]{2,1,0:T(8,128)(2,1)S(1)} %collective-permute-done.4.rest_0_, ...), custom_call_target="tpu_custom_call" | custom-call | flops 4860149760 | bytes 791040 | tf_op jit(solution)/shard_map/pallas_call | solution.py:510
  44.7 0.3 collective-permute-start.7
  45.0 0.5 collective-permute-start.8
  45.5 2.2 %collective-permute-start.9 = (f32[3,6144]{1,0:T(4,128)S(1)}, f32[3,6144]{1,0:T(4,128)S(1)}, u32[]{:S(2)}, u32[]{:S(2)}) collective-permute-start(f32[3,6144]{1,0:T(4,128)S(1)} %get-tuple-element.66), channel_id=1, source_target_pairs={{0,29},{1,30},{2,31},{3,0},{4,1},{5,2},{6,3},{7,4},{8,5},{9,6},{10... | collective-permute-start | bytes 221192 | tf_op jit(solution)/shard_map/ppermute | solution.py:49
  47.8 4.5 %shard_map.69.rest_2_ = f32[5,3,768]{2,1,0:T(4,128)S(1)} custom-call(s32[270]{0:T(512)S(1)} %get-tuple-element.38.plan_ref, bf16[4864,128]{1,0:T(8,128)(2,1)S(1)} %get-tuple-element.62.kept_ref, bf16[6,1030,128]{2,1,0:T(8,128)(2,1)S(1)} %copy-done.1, f32[3,6144]{1,0:T(4,128)S(1)} %get-tuple-element.63.before_ref), custom_call_target="tpu_custom_call" | custom-call | flops 4860149760 | bytes 791040 | tf_op jit(solution)/shard_map/pallas_call | solution.py:525
  52.3 2.4 %collective-permute-done.9.rest_5_ = f32[3,6144]{1,0:T(4,128)S(1)} collective-permute-done((f32[3,6144]{1,0:T(4,128)S(1)}, f32[3,6144]{1,0:T(4,128)S(1)}, u32[]{:S(2)}, u32[]{:S(2)}) %collective-permute-start.9) | collective-permute-done | bytes 73760 | tf_op jit(solution)/shard_map/ppermute | solution.py:49
  54.7 1.5 %shard_map.70 = f32[3,256]{1,0:T(4,128)} custom-call(s32[270]{0:T(512)S(1)} %get-tuple-element.38.plan_ref, s32[1,256]{1,0:T(1,128)S(1)} %bitcast.3, bf16[6144,128]{1,0:T(8,128)(2,1)S(1)} %shard_map.67.chosen_ref, f32[2,3,768]{2,1,0:T(4,128)S(1)} %get-tuple-element.48.rest_6_.rest_0_, f32[1,3,768]{2,1,0:T(4,128)S(1)} %get-tuple-element.49.rest_10_.rest_1_, ...), custom_call_target="tpu_custom_call" | custom-call | tf_op jit(solution)/shard_map/pallas_call | solution.py:535
  (19 shorter events, 0.1 us)
Async XLA Ops:
  0.0 0.7 %copy-start.6 = (bf16[1,24,128]{2,1,0:T(8,128)(2,1)S(1)}, bf16[1,24,128]{2,1,0:T(8,128)(2,1)}, u32[]{:S(2)}) copy-start(bf16[1,24,128]{2,1,0:T(8,128)(2,1)} %param.6) | copy-start | bytes 18436
  0.0 29.0 %copy-start.1 = (bf16[6,1030,128]{2,1,0:T(8,128)(2,1)S(1)}, bf16[6,1030,128]{2,1,0:T(8,128)(2,1)}, u32[]{:S(2)}) copy-start(bf16[6,1030,128]{2,1,0:T(8,128)(2,1)} %all_pages_ref.1) | copy-start | bytes 4746244
  0.0 29.0 %copy-start = (s32[256]{0:T(256)S(1)}, s32[256]{0:T(256)}, u32[]{:S(2)}) copy-start(s32[256]{0:T(256)} %len_hbm.1) | copy-start | bytes 3076
  0.0 29.0 %copy-start.4 = (s32[6]{0:T(128)S(1)}, s32[6]{0:T(128)}, u32[]{:S(2)}) copy-start(s32[6]{0:T(128)} %helper_hbm.1) | copy-start | bytes 76
  0.0 29.0 %copy-start.3 = (s32[3]{0:T(128)S(1)}, s32[3]{0:T(128)}, u32[]{:S(2)}) copy-start(s32[3]{0:T(128)} %offset_hbm.1) | copy-start | bytes 40
  0.0 29.0 %copy-start.2 = (s32[3]{0:T(128)S(1)}, s32[3]{0:T(128)}, u32[]{:S(2)}) copy-start(s32[3]{0:T(128)} %count_hbm.1) | copy-start | bytes 40
  22.0 7.1 %collective-permute-start.1 = (bf16[32,24,128]{2,1,0:T(8,128)(2,1)S(1)}, bf16[32,24,128]{2,1,0:T(8,128)(2,1)S(1)}, u32[]{:S(2)}, u32[]{:S(2)}) collective-permute-start(bf16[32,24,128]{2,1,0:T(8,128)(2,1)S(1)} %all_to_all.5.rest_0_), channel_id=1, source_target_pairs={{0,1},{1,0},{2,3},{3,2},{4,5},{5,4},{6,7},{7,6},{8,9},{9,8},{10,11... | collective-permute-start | bytes 589832 | tf_op jit(solution)/shard_map/ppermute | solution.py:41
  24.8 9.6 %collective-permute-start = (bf16[32,24,128]{2,1,0:T(8,128)(2,1)S(1)}, bf16[32,24,128]{2,1,0:T(8,128)(2,1)S(1)}, u32[]{:S(2)}, u32[]{:S(2)}) collective-permute-start(bf16[32,24,128]{2,1,0:T(8,128)(2,1)S(1)} %all_to_all.5.rest_0_), channel_id=1, source_target_pairs={{0,128},{1,129},{2,130},{3,131},{4,132},{5,133},{6,134},{7,135},{8... | collective-permute-start | bytes 589832 | tf_op jit(solution)/shard_map/ppermute | solution.py:36
  27.6 9.6 %collective-permute-start.3 = (bf16[32,24,128]{2,1,0:T(8,128)(2,1)S(1)}, bf16[32,24,128]{2,1,0:T(8,128)(2,1)S(1)}, u32[]{:S(2)}, u32[]{:S(2)}) collective-permute-start(bf16[32,24,128]{2,1,0:T(8,128)(2,1)S(1)} %all_to_all.5.rest_0_), channel_id=1, source_target_pairs={{0,144},{1,145},{2,146},{3,147},{4,148},{5,149},{6,150},{7,151},{8... | collective-permute-start | bytes 589832 | tf_op jit(solution)/shard_map/ppermute | solution.py:36
  28.4 8.8 %collective-permute-start.2 = (bf16[32,24,128]{2,1,0:T(8,128)(2,1)S(1)}, bf16[32,24,128]{2,1,0:T(8,128)(2,1)S(1)}, u32[]{:S(2)}, u32[]{:S(2)}) collective-permute-start(bf16[32,24,128]{2,1,0:T(8,128)(2,1)S(1)} %all_to_all.5.rest_0_), channel_id=1, source_target_pairs={{0,16},{1,17},{2,18},{3,19},{4,20},{5,21},{6,22},{7,23},{8,24},{9,... | collective-permute-start | bytes 589832 | tf_op jit(solution)/shard_map/ppermute | solution.py:36
  37.2 2.5 %collective-permute-start.4 = (bf16[32,24,128]{2,1,0:T(8,128)(2,1)S(1)}, bf16[32,24,128]{2,1,0:T(8,128)(2,1)S(1)}, u32[]{:S(2)}, u32[]{:S(2)}) collective-permute-start(bf16[32,24,128]{2,1,0:T(8,128)(2,1)S(1)} %collective-permute-done.rest_0_), channel_id=1, source_target_pairs={{0,1},{1,0},{2,3},{3,2},{4,5},{5,4},{6,7},{7,6},{8,9},{9,8},{10,11... | collective-permute-start | bytes 589832 | tf_op jit(solution)/shard_map/ppermute | solution.py:41
  38.0 1.7 %collective-permute-start.5 = (bf16[32,24,128]{2,1,0:T(8,128)(2,1)S(1)}, bf16[32,24,128]{2,1,0:T(8,128)(2,1)S(1)}, u32[]{:S(2)}, u32[]{:S(2)}) collective-permute-start(bf16[32,24,128]{2,1,0:T(8,128)(2,1)S(1)} %collective-permute-done.2.rest_1_), channel_id=1, source_target_pairs={{0,1},{1,0},{2,3},{3,2},{4,5},{5,4},{6,7},{7,6},{8,9},{9,8},{10,11... | collective-permute-start | bytes 589832 | tf_op jit(solution)/shard_map/ppermute | solution.py:41
  38.0 1.7 %collective-permute-start.6 = (bf16[32,24,128]{2,1,0:T(8,128)(2,1)S(1)}, bf16[32,24,128]{2,1,0:T(8,128)(2,1)S(1)}, u32[]{:S(2)}, u32[]{:S(2)}) collective-permute-start(bf16[32,24,128]{2,1,0:T(8,128)(2,1)S(1)} %collective-permute-done.3.rest_3_), channel_id=1, source_target_pairs={{0,1},{1,0},{2,3},{3,2},{4,5},{5,4},{6,7},{7,6},{8,9},{9,8},{10,11... | collective-permute-start | bytes 589832 | tf_op jit(solution)/shard_map/ppermute | solution.py:41
  38.5 1.2 %copy-start.5 = (f32[8,128]{1,0:T(8,128)S(1)}, f32[8,128]{1,0:T(8,128)}, u32[]{:S(2)}) copy-start(f32[8,128]{1,0:T(8,128)} %shard_map.64.nothing_ref) | copy-start | bytes 12292
  44.7 7.6 %collective-permute-start.7 = (f32[3,6144]{1,0:T(4,128)S(1)}, f32[3,6144]{1,0:T(4,128)S(1)}, u32[]{:S(2)}, u32[]{:S(2)}) collective-permute-start(f32[3,6144]{1,0:T(4,128)S(1)} %get-tuple-element.64), channel_id=1, source_target_pairs={{0,31},{1,0},{2,1},{3,2},{4,3},{5,4},{6,5},{7,6},{8,7},{9,8},{10,9... | collective-permute-start | bytes 221192 | tf_op jit(solution)/shard_map/ppermute | solution.py:49
  45.0 7.3 %collective-permute-start.8 = (f32[3,6144]{1,0:T(4,128)S(1)}, f32[3,6144]{1,0:T(4,128)S(1)}, u32[]{:S(2)}, u32[]{:S(2)}) collective-permute-start(f32[3,6144]{1,0:T(4,128)S(1)} %get-tuple-element.65), channel_id=1, source_target_pairs={{0,30},{1,31},{2,0},{3,1},{4,2},{5,3},{6,4},{7,5},{8,6},{9,7},{10,... | collective-permute-start | bytes 221192 | tf_op jit(solution)/shard_map/ppermute | solution.py:49
  45.5 9.1 %collective-permute-start.9 = (f32[3,6144]{1,0:T(4,128)S(1)}, f32[3,6144]{1,0:T(4,128)S(1)}, u32[]{:S(2)}, u32[]{:S(2)}) collective-permute-start(f32[3,6144]{1,0:T(4,128)S(1)} %get-tuple-element.66), channel_id=1, source_target_pairs={{0,29},{1,30},{2,31},{3,0},{4,1},{5,2},{6,3},{7,4},{8,5},{9,6},{10... | collective-permute-start | bytes 221192 | tf_op jit(solution)/shard_map/ppermute | solution.py:49

commit v4 on v3

--- a/solution.py
+++ b/solution.py
@@ -8,6 +8,7 @@
 from jax.sharding import Mesh, PartitionSpec as P
 
 SPILL = 3
+SEND_ORDER = (3, 1, 2)
 SIZES = (2, 4, 2, 8, 2)
 AXES = ("xh", "y", "xl", "z", "c")
 NX, NY, NZ, NC = 4, 4, 8, 2
@@ -520,7 +521,7 @@
         compiler_params=params,
         cost_estimate=cost((pages.shape[0] - docs) * pages.shape[1]),
     )(plan, nothing, *arrived, pages, *own_out, *far_out)
-    received = [along_blk(partials[distance], -distance) for distance in range(1, SPILL + 1)]
+    received = [along_blk(partials[distance], -distance) for distance in SEND_ORDER]
 
     rest_home = pl.pallas_call(
         functools.partial(home_kernel, rest, total),

time: 56.3 us -> 54.9 us (0.975)
  waiting for transfers between devices: 2.67 us -> 1 us
    ppermute x3, waiting for transfers between devices: 2.36 us -> 0.7 us  [along_blk(): return lax.ppermute(value, AXES, pairs)]
  transfers between devices with their start and end apart: 10 -> 10, of which waited for: 2 -> 3; matrix products, arithmetic and copies ran while one was open for 0% -> 0% of each run, Pallas kernels for 24% -> 25%
where the time goes in v4:
time: 54.9 us; the launch traced here: 54.7 us
  blocking collectives  21.2 us (39%)
  Pallas kernels  20.6 us (38%)
  starting transfers between devices  11.6 us (21%)
  waiting for transfers between devices  1 us (2%)
    all_to_all x1, blocking collectives, local(): mine = lax.all_to_all(copies, ('y', 'z'), 0, 0, tiled=True)  21.2 us
    pallas_call x1, Pallas kernels, local(): pl.pallas_call(functools.partial(first_kernel, own), out_shape=part(own)...  5.32 us
    pallas_call x1, Pallas kernels, local(): pl.pallas_call(functools.partial(late_kernel, rest, (own, far), total), o...  4.98 us
    pallas_call x1, Pallas kernels, local(): pl.pallas_call(functools.partial(home_kernel, rest, total), out_shape=par...  4.53 us
    ppermute x3, starting transfers between devices, along_x(): return lax.ppermute(value, AXES, pairs)  4.21 us
    ppermute x4, starting transfers between devices, other_core(): return lax.ppermute(value, AXES, pairs)  4.14 us
    ppermute x3, starting transfers between devices, along_blk(): return lax.ppermute(value, AXES, pairs)  3.27 us
    pallas_call x1, Pallas kernels, local(): pl.pallas_call(functools.partial(more_kernel, far, total), out_shape=part...  2.51 us
  transfers between devices with their start and end apart: 10, of which 3 were waited for; matrix products, arithmetic and copies ran while one was open for 0% of the time, Pallas kernels for 25%

profile of v4, /device:TPU:1, one launch (start us, length us, event | category | flops | bytes accessed | tf_op | source)
XLA Modules:
  0.0 54.7 jit_solution(14038989971769277754)
XLA Ops:
  0.0 0.6 %shard_map.64.nothing_ref = f32[8,128]{1,0:T(8,128)} custom-call(), custom_call_target="tpu_custom_call" | custom-call | flops 9720299520 | bytes 1582080 | tf_op jit(solution)/shard_map/pallas_call | solution.py:455
  0.6 0.1 copy-done.6
  0.7 21.2 %all_to_all.5.rest_0_ = bf16[32,24,128]{2,1,0:T(8,128)(2,1)S(1)} all-to-all(bf16[32,24,128]{2,1,0:T(8,128)(2,1)S(1)} %broadcast_in_dim.11), channel_id=1, replica_groups=mesh['xh'=2,'y'=4,'xl'=2,'z'=8,'c'=2] {'y','z'}, dimensions={0} | all-to-all | bytes 393216 | tf_op jit(solution)/shard_map/all_to_all | solution.py:463
  22.0 2.8 %collective-permute-start.1 = (bf16[32,24,128]{2,1,0:T(8,128)(2,1)S(1)}, bf16[32,24,128]{2,1,0:T(8,128)(2,1)S(1)}, u32[]{:S(2)}, u32[]{:S(2)}) collective-permute-start(bf16[32,24,128]{2,1,0:T(8,128)(2,1)S(1)} %all_to_all.5.rest_0_), channel_id=1, source_target_pairs={{0,1},{1,0},{2,3},{3,2},{4,5},{5,4},{6,7},{7,6},{8,9},{9,8},{10,11... | collective-permute-start | bytes 589832 | tf_op jit(solution)/shard_map/ppermute | solution.py:42
  24.8 2.7 %collective-permute-start = (bf16[32,24,128]{2,1,0:T(8,128)(2,1)S(1)}, bf16[32,24,128]{2,1,0:T(8,128)(2,1)S(1)}, u32[]{:S(2)}, u32[]{:S(2)}) collective-permute-start(bf16[32,24,128]{2,1,0:T(8,128)(2,1)S(1)} %all_to_all.5.rest_0_), channel_id=1, source_target_pairs={{0,128},{1,129},{2,130},{3,131},{4,132},{5,133},{6,134},{7,135},{8... | collective-permute-start | bytes 589832 | tf_op jit(solution)/shard_map/ppermute | solution.py:37
  27.6 0.9 %collective-permute-start.3 = (bf16[32,24,128]{2,1,0:T(8,128)(2,1)S(1)}, bf16[32,24,128]{2,1,0:T(8,128)(2,1)S(1)}, u32[]{:S(2)}, u32[]{:S(2)}) collective-permute-start(bf16[32,24,128]{2,1,0:T(8,128)(2,1)S(1)} %all_to_all.5.rest_0_), channel_id=1, source_target_pairs={{0,144},{1,145},{2,146},{3,147},{4,148},{5,149},{6,150},{7,151},{8... | collective-permute-start | bytes 589832 | tf_op jit(solution)/shard_map/ppermute | solution.py:37
  28.4 0.6 %collective-permute-start.2 = (bf16[32,24,128]{2,1,0:T(8,128)(2,1)S(1)}, bf16[32,24,128]{2,1,0:T(8,128)(2,1)S(1)}, u32[]{:S(2)}, u32[]{:S(2)}) collective-permute-start(bf16[32,24,128]{2,1,0:T(8,128)(2,1)S(1)} %all_to_all.5.rest_0_), channel_id=1, source_target_pairs={{0,16},{1,17},{2,18},{3,19},{4,20},{5,21},{6,22},{7,23},{8,24},{9,... | collective-permute-start | bytes 589832 | tf_op jit(solution)/shard_map/ppermute | solution.py:37
  29.1 5.3 %shard_map.65 = (f32[2,3,768]{2,1,0:T(4,128)S(1)}, f32[2,3,768]{2,1,0:T(4,128)S(1)}, f32[2,3,768]{2,1,0:T(4,128)S(1)}, f32[2,3,768]{2,1,0:T(4,128)S(1)}, s32[270]{0:T(512)S(1)}) custom-call(s32[256]{0:T(256)S(1)} %copy-done, s32[3]{0:T(128)S(1)} %copy-done.2, s32[3]{0:T(128)S(1)} %copy-done.3, s32[6]{0:T(128)S(1)} %copy-done.4, ...), custom_call_target="tpu_custom_call" | custom-call | flops 1101004800 | bytes 179200 | tf_op jit(solution)/shard_map/pallas_call | solution.py:467
  34.4 0.0 collective-permute-done.rest_0_
  34.4 2.5 %shard_map.66 = (f32[1,3,768]{2,1,0:T(4,128)S(1)}, f32[1,3,768]{2,1,0:T(4,128)S(1)}, f32[1,3,768]{2,1,0:T(4,128)S(1)}, f32[1,3,768]{2,1,0:T(4,128)S(1)}) custom-call(s32[270]{0:T(512)S(1)} %get-tuple-element.38.plan_ref, bf16[32,24,128]{2,1,0:T(8,128)(2,1)S(1)} %collective-permute-done.rest_0_, bf16[6,1030,128]{2,1,0:T(8,128)(2,1)S(1)} %copy-done.1), custom_call_target="tpu_custom_call" | custom-call | flops 1101004800 | bytes 179200 | tf_op jit(solution)/shard_map/pallas_call | solution.py:488
  36.9 0.3 collective-permute-done.3.rest_3_
  37.2 0.8 %collective-permute-start.4 = (bf16[32,24,128]{2,1,0:T(8,128)(2,1)S(1)}, bf16[32,24,128]{2,1,0:T(8,128)(2,1)S(1)}, u32[]{:S(2)}, u32[]{:S(2)}) collective-permute-start(bf16[32,24,128]{2,1,0:T(8,128)(2,1)S(1)} %collective-permute-done.rest_0_), channel_id=1, source_target_pairs={{0,1},{1,0},{2,3},{3,2},{4,5},{5,4},{6,7},{7,6},{8,9},{9,8},{10,11... | collective-permute-start | bytes 589832 | tf_op jit(solution)/shard_map/ppermute | solution.py:42
  38.0 0.0 collective-permute-start.5
  38.0 0.5 collective-permute-start.6
  38.5 1.2 %shard_map.67.chosen_ref = bf16[6144,128]{1,0:T(8,128)(2,1)S(1)} custom-call(s32[270]{0:T(512)S(1)} %get-tuple-element.38.plan_ref, s32[1,256]{1,0:T(1,128)S(1)} %bitcast.2), custom_call_target="tpu_custom_call" | custom-call | flops 1620049920 | bytes 263680 | tf_op jit(solution)/shard_map/pallas_call | solution.py:500
  39.7 0.0 collective-permute-done.4.rest_0_
  39.7 0.0 collective-permute-done.6.rest_4_
  39.7 5.0 %shard_map.68 = (f32[3,6144]{1,0:T(4,128)S(1)}, f32[3,6144]{1,0:T(4,128)S(1)}, f32[3,6144]{1,0:T(4,128)S(1)}, f32[3,6144]{1,0:T(4,128)S(1)}, bf16[4864,128]{1,0:T(8,128)(2,1)S(1)}) custom-call(s32[270]{0:T(512)S(1)} %get-tuple-element.38.plan_ref, f32[8,128]{1,0:T(8,128)S(1)} %copy-done.5, bf16[32,24,128]{2,1,0:T(8,128)(2,1)S(1)} %collective-permute-done.4.rest_0_, ...), custom_call_target="tpu_custom_call" | custom-call | flops 4860149760 | bytes 791040 | tf_op jit(solution)/shard_map/pallas_call | solution.py:511
  44.7 0.7 %collective-permute-start.7 = (f32[3,6144]{1,0:T(4,128)S(1)}, f32[3,6144]{1,0:T(4,128)S(1)}, u32[]{:S(2)}, u32[]{:S(2)}) collective-permute-start(f32[3,6144]{1,0:T(4,128)S(1)} %get-tuple-element.64), channel_id=1, source_target_pairs={{0,29},{1,30},{2,31},{3,0},{4,1},{5,2},{6,3},{7,4},{8,5},{9,6},{10... | collective-permute-start | bytes 221192 | tf_op jit(solution)/shard_map/ppermute | solution.py:50
  45.4 2.5 %collective-permute-start.8 = (f32[3,6144]{1,0:T(4,128)S(1)}, f32[3,6144]{1,0:T(4,128)S(1)}, u32[]{:S(2)}, u32[]{:S(2)}) collective-permute-start(f32[3,6144]{1,0:T(4,128)S(1)} %get-tuple-element.65), channel_id=1, source_target_pairs={{0,31},{1,0},{2,1},{3,2},{4,3},{5,4},{6,5},{7,6},{8,7},{9,8},{10,9... | collective-permute-start | bytes 221192 | tf_op jit(solution)/shard_map/ppermute | solution.py:50
  48.0 4.5 %shard_map.69.rest_2_ = f32[5,3,768]{2,1,0:T(4,128)S(1)} custom-call(s32[270]{0:T(512)S(1)} %get-tuple-element.38.plan_ref, bf16[4864,128]{1,0:T(8,128)(2,1)S(1)} %get-tuple-element.62.kept_ref, bf16[6,1030,128]{2,1,0:T(8,128)(2,1)S(1)} %copy-done.1, f32[3,6144]{1,0:T(4,128)S(1)} %get-tuple-element.63.before_ref), custom_call_target="tpu_custom_call" | custom-call | flops 4860149760 | bytes 791040 | tf_op jit(solution)/shard_map/pallas_call | solution.py:526
  52.5 0.2 collective-permute-done.8.rest_4_
  52.7 0.5 collective-permute-done.9.rest_5_
  53.2 1.5 %shard_map.70 = f32[3,256]{1,0:T(4,128)} custom-call(s32[270]{0:T(512)S(1)} %get-tuple-element.38.plan_ref, s32[1,256]{1,0:T(1,128)S(1)} %bitcast.3, bf16[6144,128]{1,0:T(8,128)(2,1)S(1)} %shard_map.67.chosen_ref, f32[2,3,768]{2,1,0:T(4,128)S(1)} %get-tuple-element.48.rest_6_.rest_0_, f32[1,3,768]{2,1,0:T(4,128)S(1)} %get-tuple-element.49.rest_10_.rest_1_, ...), custom_call_target="tpu_custom_call" | custom-call | tf_op jit(solution)/shard_map/pallas_call | solution.py:536
  (19 shorter events, 0.1 us)
Async XLA Ops:
  0.0 0.7 %copy-start.6 = (bf16[1,24,128]{2,1,0:T(8,128)(2,1)S(1)}, bf16[1,24,128]{2,1,0:T(8,128)(2,1)}, u32[]{:S(2)}) copy-start(bf16[1,24,128]{2,1,0:T(8,128)(2,1)} %param.6) | copy-start | bytes 18436
  0.0 29.0 %copy-start.1 = (bf16[6,1030,128]{2,1,0:T(8,128)(2,1)S(1)}, bf16[6,1030,128]{2,1,0:T(8,128)(2,1)}, u32[]{:S(2)}) copy-start(bf16[6,1030,128]{2,1,0:T(8,128)(2,1)} %all_pages_ref.1) | copy-start | bytes 4746244
  0.0 29.0 %copy-start = (s32[256]{0:T(256)S(1)}, s32[256]{0:T(256)}, u32[]{:S(2)}) copy-start(s32[256]{0:T(256)} %len_hbm.1) | copy-start | bytes 3076
  0.0 29.0 %copy-start.4 = (s32[6]{0:T(128)S(1)}, s32[6]{0:T(128)}, u32[]{:S(2)}) copy-start(s32[6]{0:T(128)} %helper_hbm.1) | copy-start | bytes 76
  0.0 29.0 %copy-start.3 = (s32[3]{0:T(128)S(1)}, s32[3]{0:T(128)}, u32[]{:S(2)}) copy-start(s32[3]{0:T(128)} %offset_hbm.1) | copy-start | bytes 40
  0.0 29.0 %copy-start.2 = (s32[3]{0:T(128)S(1)}, s32[3]{0:T(128)}, u32[]{:S(2)}) copy-start(s32[3]{0:T(128)} %count_hbm.1) | copy-start | bytes 40
  22.0 7.1 %collective-permute-start.1 = (bf16[32,24,128]{2,1,0:T(8,128)(2,1)S(1)}, bf16[32,24,128]{2,1,0:T(8,128)(2,1)S(1)}, u32[]{:S(2)}, u32[]{:S(2)}) collective-permute-start(bf16[32,24,128]{2,1,0:T(8,128)(2,1)S(1)} %all_to_all.5.rest_0_), channel_id=1, source_target_pairs={{0,1},{1,0},{2,3},{3,2},{4,5},{5,4},{6,7},{7,6},{8,9},{9,8},{10,11... | collective-permute-start | bytes 589832 | tf_op jit(solution)/shard_map/ppermute | solution.py:42
  24.8 9.6 %collective-permute-start = (bf16[32,24,128]{2,1,0:T(8,128)(2,1)S(1)}, bf16[32,24,128]{2,1,0:T(8,128)(2,1)S(1)}, u32[]{:S(2)}, u32[]{:S(2)}) collective-permute-start(bf16[32,24,128]{2,1,0:T(8,128)(2,1)S(1)} %all_to_all.5.rest_0_), channel_id=1, source_target_pairs={{0,128},{1,129},{2,130},{3,131},{4,132},{5,133},{6,134},{7,135},{8... | collective-permute-start | bytes 589832 | tf_op jit(solution)/shard_map/ppermute | solution.py:37
  27.6 9.6 %collective-permute-start.3 = (bf16[32,24,128]{2,1,0:T(8,128)(2,1)S(1)}, bf16[32,24,128]{2,1,0:T(8,128)(2,1)S(1)}, u32[]{:S(2)}, u32[]{:S(2)}) collective-permute-start(bf16[32,24,128]{2,1,0:T(8,128)(2,1)S(1)} %all_to_all.5.rest_0_), channel_id=1, source_target_pairs={{0,144},{1,145},{2,146},{3,147},{4,148},{5,149},{6,150},{7,151},{8... | collective-permute-start | bytes 589832 | tf_op jit(solution)/shard_map/ppermute | solution.py:37
  28.4 8.8 %collective-permute-start.2 = (bf16[32,24,128]{2,1,0:T(8,128)(2,1)S(1)}, bf16[32,24,128]{2,1,0:T(8,128)(2,1)S(1)}, u32[]{:S(2)}, u32[]{:S(2)}) collective-permute-start(bf16[32,24,128]{2,1,0:T(8,128)(2,1)S(1)} %all_to_all.5.rest_0_), channel_id=1, source_target_pairs={{0,16},{1,17},{2,18},{3,19},{4,20},{5,21},{6,22},{7,23},{8,24},{9,... | collective-permute-start | bytes 589832 | tf_op jit(solution)/shard_map/ppermute | solution.py:37
  37.2 2.5 %collective-permute-start.4 = (bf16[32,24,128]{2,1,0:T(8,128)(2,1)S(1)}, bf16[32,24,128]{2,1,0:T(8,128)(2,1)S(1)}, u32[]{:S(2)}, u32[]{:S(2)}) collective-permute-start(bf16[32,24,128]{2,1,0:T(8,128)(2,1)S(1)} %collective-permute-done.rest_0_), channel_id=1, source_target_pairs={{0,1},{1,0},{2,3},{3,2},{4,5},{5,4},{6,7},{7,6},{8,9},{9,8},{10,11... | collective-permute-start | bytes 589832 | tf_op jit(solution)/shard_map/ppermute | solution.py:42
  38.0 1.7 %collective-permute-start.5 = (bf16[32,24,128]{2,1,0:T(8,128)(2,1)S(1)}, bf16[32,24,128]{2,1,0:T(8,128)(2,1)S(1)}, u32[]{:S(2)}, u32[]{:S(2)}) collective-permute-start(bf16[32,24,128]{2,1,0:T(8,128)(2,1)S(1)} %collective-permute-done.2.rest_1_), channel_id=1, source_target_pairs={{0,1},{1,0},{2,3},{3,2},{4,5},{5,4},{6,7},{7,6},{8,9},{9,8},{10,11... | collective-permute-start | bytes 589832 | tf_op jit(solution)/shard_map/ppermute | solution.py:42
  38.0 1.7 %collective-permute-start.6 = (bf16[32,24,128]{2,1,0:T(8,128)(2,1)S(1)}, bf16[32,24,128]{2,1,0:T(8,128)(2,1)S(1)}, u32[]{:S(2)}, u32[]{:S(2)}) collective-permute-start(bf16[32,24,128]{2,1,0:T(8,128)(2,1)S(1)} %collective-permute-done.3.rest_3_), channel_id=1, source_target_pairs={{0,1},{1,0},{2,3},{3,2},{4,5},{5,4},{6,7},{7,6},{8,9},{9,8},{10,11... | collective-permute-start | bytes 589832 | tf_op jit(solution)/shard_map/ppermute | solution.py:42
  38.5 1.2 %copy-start.5 = (f32[8,128]{1,0:T(8,128)S(1)}, f32[8,128]{1,0:T(8,128)}, u32[]{:S(2)}) copy-start(f32[8,128]{1,0:T(8,128)} %shard_map.64.nothing_ref) | copy-start | bytes 12292
  44.7 7.8 %collective-permute-start.7 = (f32[3,6144]{1,0:T(4,128)S(1)}, f32[3,6144]{1,0:T(4,128)S(1)}, u32[]{:S(2)}, u32[]{:S(2)}) collective-permute-start(f32[3,6144]{1,0:T(4,128)S(1)} %get-tuple-element.64), channel_id=1, source_target_pairs={{0,29},{1,30},{2,31},{3,0},{4,1},{5,2},{6,3},{7,4},{8,5},{9,6},{10... | collective-permute-start | bytes 221192 | tf_op jit(solution)/shard_map/ppermute | solution.py:50
  45.4 7.2 %collective-permute-start.8 = (f32[3,6144]{1,0:T(4,128)S(1)}, f32[3,6144]{1,0:T(4,128)S(1)}, u32[]{:S(2)}, u32[]{:S(2)}) collective-permute-start(f32[3,6144]{1,0:T(4,128)S(1)} %get-tuple-element.65), channel_id=1, source_target_pairs={{0,31},{1,0},{2,1},{3,2},{4,3},{5,4},{6,5},{7,6},{8,7},{9,8},{10,9... | collective-permute-start | bytes 221192 | tf_op jit(solution)/shard_map/ppermute | solution.py:50
  48.0 5.2 %collective-permute-start.9 = (f32[3,6144]{1,0:T(4,128)S(1)}, f32[3,6144]{1,0:T(4,128)S(1)}, u32[]{:S(2)}, u32[]{:S(2)}) collective-permute-start(f32[3,6144]{1,0:T(4,128)S(1)} %get-tuple-element.66), channel_id=1, source_target_pairs={{0,30},{1,31},{2,0},{3,1},{4,2},{5,3},{6,4},{7,5},{8,6},{9,7},{10,... | collective-permute-start | bytes 221192 | tf_op jit(solution)/shard_map/ppermute | solution.py:50

commit v5 on v4

--- a/solution.py
+++ b/solution.py
@@ -462,7 +462,7 @@
     copies = jnp.broadcast_to(queries, (CHUNK, tokens, width))
     mine = lax.all_to_all(copies, ("y", "z"), 0, 0, tiled=True)
     mine_other = other_core(mine)
-    two, one, three = [along_x(mine, steps) for steps in (2, 1, 3)]
+    two, three, one = [along_x(mine, steps) for steps in (2, 3, 1)]
 
     *own_out, plan = pl.pallas_call(
         functools.partial(first_kernel, own),

time: 54.9 us -> 54.7 us (level)
  Pallas kernels: 20.6 us -> 21.8 us
  starting transfers between devices: 11.6 us -> 11 us
    pallas_call x1, Pallas kernels: 4.98 us -> 5.58 us  [local(): pl.pallas_call(functools.partial(late_kernel, rest, (own, far), total), o...]
    ppermute x3, starting transfers between devices: 3.27 us -> 2.67 us  [along_blk(): return lax.ppermute(value, AXES, pairs)]
    pallas_call x1, Pallas kernels: 4.53 us -> 5.13 us  [local(): pl.pallas_call(functools.partial(home_kernel, rest, total), out_shape=par...]
  transfers between devices with their start and end apart: 10 -> 10, of which waited for: 3 -> 2; matrix products, arithmetic and copies ran while one was open for 0% -> 0% of each run, Pallas kernels for 25% -> 26%
where the time goes in v5:
time: 54.7 us; the launch traced here: 54.8 us
  Pallas kernels  21.8 us (40%)
  blocking collectives  21.2 us (39%)
  starting transfers between devices  11 us (20%)
    all_to_all x1, blocking collectives, local(): mine = lax.all_to_all(copies, ('y', 'z'), 0, 0, tiled=True)  21.2 us
    pallas_call x1, Pallas kernels, local(): pl.pallas_call(functools.partial(late_kernel, rest, (own, far), total), o...  5.58 us
    pallas_call x1, Pallas kernels, local(): pl.pallas_call(functools.partial(first_kernel, own), out_shape=part(own)...  5.32 us
    pallas_call x1, Pallas kernels, local(): pl.pallas_call(functools.partial(home_kernel, rest, total), out_shape=par...  5.13 us
    ppermute x3, starting transfers between devices, along_x(): return lax.ppermute(value, AXES, pairs)  4.21 us
    ppermute x4, starting transfers between devices, other_core(): return lax.ppermute(value, AXES, pairs)  4.14 us
    ppermute x3, starting transfers between devices, along_blk(): return lax.ppermute(value, AXES, pairs)  2.67 us
    pallas_call x1, Pallas kernels, local(): pl.pallas_call(functools.partial(more_kernel, far, total), out_shape=part...  2.5 us
  transfers between devices with their start and end apart: 10, of which 2 were waited for; matrix products, arithmetic and copies ran while one was open for 0% of the time, Pallas kernels for 26%

profile of v5, /device:TPU:1, one launch (start us, length us, event | category | flops | bytes accessed | tf_op | source)
XLA Modules:
  0.0 54.8 jit_solution(14038989971769277754)
XLA Ops:
  0.0 0.6 %shard_map.64.nothing_ref = f32[8,128]{1,0:T(8,128)} custom-call(), custom_call_target="tpu_custom_call" | custom-call | flops 9720299520 | bytes 1582080 | tf_op jit(solution)/shard_map/pallas_call | solution.py:455
  0.6 0.1 copy-done.6
  0.7 21.2 %all_to_all.5.rest_0_ = bf16[32,24,128]{2,1,0:T(8,128)(2,1)S(1)} all-to-all(bf16[32,24,128]{2,1,0:T(8,128)(2,1)S(1)} %broadcast_in_dim.11), channel_id=1, replica_groups=mesh['xh'=2,'y'=4,'xl'=2,'z'=8,'c'=2] {'y','z'}, dimensions={0} | all-to-all | bytes 393216 | tf_op jit(solution)/shard_map/all_to_all | solution.py:463
  22.0 2.8 %collective-permute-start.1 = (bf16[32,24,128]{2,1,0:T(8,128)(2,1)S(1)}, bf16[32,24,128]{2,1,0:T(8,128)(2,1)S(1)}, u32[]{:S(2)}, u32[]{:S(2)}) collective-permute-start(bf16[32,24,128]{2,1,0:T(8,128)(2,1)S(1)} %all_to_all.5.rest_0_), channel_id=1, source_target_pairs={{0,1},{1,0},{2,3},{3,2},{4,5},{5,4},{6,7},{7,6},{8,9},{9,8},{10,11... | collective-permute-start | bytes 589832 | tf_op jit(solution)/shard_map/ppermute | solution.py:42
  24.8 2.7 %collective-permute-start = (bf16[32,24,128]{2,1,0:T(8,128)(2,1)S(1)}, bf16[32,24,128]{2,1,0:T(8,128)(2,1)S(1)}, u32[]{:S(2)}, u32[]{:S(2)}) collective-permute-start(bf16[32,24,128]{2,1,0:T(8,128)(2,1)S(1)} %all_to_all.5.rest_0_), channel_id=1, source_target_pairs={{0,128},{1,129},{2,130},{3,131},{4,132},{5,133},{6,134},{7,135},{8... | collective-permute-start | bytes 589832 | tf_op jit(solution)/shard_map/ppermute | solution.py:37
  27.6 0.9 %collective-permute-start.3 = (bf16[32,24,128]{2,1,0:T(8,128)(2,1)S(1)}, bf16[32,24,128]{2,1,0:T(8,128)(2,1)S(1)}, u32[]{:S(2)}, u32[]{:S(2)}) collective-permute-start(bf16[32,24,128]{2,1,0:T(8,128)(2,1)S(1)} %all_to_all.5.rest_0_), channel_id=1, source_target_pairs={{0,144},{1,145},{2,146},{3,147},{4,148},{5,149},{6,150},{7,151},{8... | collective-permute-start | bytes 589832 | tf_op jit(solution)/shard_map/ppermute | solution.py:37
  28.4 0.6 %collective-permute-start.2 = (bf16[32,24,128]{2,1,0:T(8,128)(2,1)S(1)}, bf16[32,24,128]{2,1,0:T(8,128)(2,1)S(1)}, u32[]{:S(2)}, u32[]{:S(2)}) collective-permute-start(bf16[32,24,128]{2,1,0:T(8,128)(2,1)S(1)} %all_to_all.5.rest_0_), channel_id=1, source_target_pairs={{0,16},{1,17},{2,18},{3,19},{4,20},{5,21},{6,22},{7,23},{8,24},{9,... | collective-permute-start | bytes 589832 | tf_op jit(solution)/shard_map/ppermute | solution.py:37
  29.0 0.0 collective-permute-done.1.rest_1_
  29.1 5.3 %shard_map.65 = (f32[2,3,768]{2,1,0:T(4,128)S(1)}, f32[2,3,768]{2,1,0:T(4,128)S(1)}, f32[2,3,768]{2,1,0:T(4,128)S(1)}, f32[2,3,768]{2,1,0:T(4,128)S(1)}, s32[270]{0:T(512)S(1)}) custom-call(s32[256]{0:T(256)S(1)} %copy-done, s32[3]{0:T(128)S(1)} %copy-done.2, s32[3]{0:T(128)S(1)} %copy-done.3, s32[6]{0:T(128)S(1)} %copy-done.4, ...), custom_call_target="tpu_custom_call" | custom-call | flops 1101004800 | bytes 179200 | tf_op jit(solution)/shard_map/pallas_call | solution.py:467
  34.4 0.0 collective-permute-done.rest_0_
  34.4 2.5 %shard_map.66 = (f32[1,3,768]{2,1,0:T(4,128)S(1)}, f32[1,3,768]{2,1,0:T(4,128)S(1)}, f32[1,3,768]{2,1,0:T(4,128)S(1)}, f32[1,3,768]{2,1,0:T(4,128)S(1)}) custom-call(s32[270]{0:T(512)S(1)} %get-tuple-element.38.plan_ref, bf16[32,24,128]{2,1,0:T(8,128)(2,1)S(1)} %collective-permute-done.rest_0_, bf16[6,1030,128]{2,1,0:T(8,128)(2,1)S(1)} %copy-done.1), custom_call_target="tpu_custom_call" | custom-call | flops 1101004800 | bytes 179200 | tf_op jit(solution)/shard_map/pallas_call | solution.py:488
  36.9 0.3 collective-permute-done.3.rest_3_
  37.2 0.8 %collective-permute-start.4 = (bf16[32,24,128]{2,1,0:T(8,128)(2,1)S(1)}, bf16[32,24,128]{2,1,0:T(8,128)(2,1)S(1)}, u32[]{:S(2)}, u32[]{:S(2)}) collective-permute-start(bf16[32,24,128]{2,1,0:T(8,128)(2,1)S(1)} %collective-permute-done.rest_0_), channel_id=1, source_target_pairs={{0,1},{1,0},{2,3},{3,2},{4,5},{5,4},{6,7},{7,6},{8,9},{9,8},{10,11... | collective-permute-start | bytes 589832 | tf_op jit(solution)/shard_map/ppermute | solution.py:42
  38.0 0.0 collective-permute-start.5
  38.0 0.5 collective-permute-start.6
  38.5 1.2 %shard_map.67.chosen_ref = bf16[6144,128]{1,0:T(8,128)(2,1)S(1)} custom-call(s32[270]{0:T(512)S(1)} %get-tuple-element.38.plan_ref, s32[1,256]{1,0:T(1,128)S(1)} %bitcast.2), custom_call_target="tpu_custom_call" | custom-call | flops 1620049920 | bytes 263680 | tf_op jit(solution)/shard_map/pallas_call | solution.py:500
  39.7 0.0 collective-permute-done.6.rest_4_
  39.7 5.6 %shard_map.68 = (f32[3,6144]{1,0:T(4,128)S(1)}, f32[3,6144]{1,0:T(4,128)S(1)}, f32[3,6144]{1,0:T(4,128)S(1)}, f32[3,6144]{1,0:T(4,128)S(1)}, bf16[4864,128]{1,0:T(8,128)(2,1)S(1)}) custom-call(s32[270]{0:T(512)S(1)} %get-tuple-element.38.plan_ref, f32[8,128]{1,0:T(8,128)S(1)} %copy-done.5, bf16[32,24,128]{2,1,0:T(8,128)(2,1)S(1)} %collective-permute-done.4.rest_0_, ...), custom_call_target="tpu_custom_call" | custom-call | flops 4860149760 | bytes 791040 | tf_op jit(solution)/shard_map/pallas_call | solution.py:511
  45.3 0.1 collective-permute-start.7
  45.4 2.5 %collective-permute-start.8 = (f32[3,6144]{1,0:T(4,128)S(1)}, f32[3,6144]{1,0:T(4,128)S(1)}, u32[]{:S(2)}, u32[]{:S(2)}) collective-permute-start(f32[3,6144]{1,0:T(4,128)S(1)} %get-tuple-element.65), channel_id=1, source_target_pairs={{0,31},{1,0},{2,1},{3,2},{4,3},{5,4},{6,5},{7,6},{8,7},{9,8},{10,9... | collective-permute-start | bytes 221192 | tf_op jit(solution)/shard_map/ppermute | solution.py:50
  48.0 0.0 collective-permute-start.9
  48.0 5.1 %shard_map.69.rest_2_ = f32[5,3,768]{2,1,0:T(4,128)S(1)} custom-call(s32[270]{0:T(512)S(1)} %get-tuple-element.38.plan_ref, bf16[4864,128]{1,0:T(8,128)(2,1)S(1)} %get-tuple-element.62.kept_ref, bf16[6,1030,128]{2,1,0:T(8,128)(2,1)S(1)} %copy-done.1, f32[3,6144]{1,0:T(4,128)S(1)} %get-tuple-element.63.before_ref), custom_call_target="tpu_custom_call" | custom-call | flops 4860149760 | bytes 791040 | tf_op jit(solution)/shard_map/pallas_call | solution.py:526
  53.1 0.1 collective-permute-done.9.rest_5_
  53.3 1.5 %shard_map.70 = f32[3,256]{1,0:T(4,128)} custom-call(s32[270]{0:T(512)S(1)} %get-tuple-element.38.plan_ref, s32[1,256]{1,0:T(1,128)S(1)} %bitcast.3, bf16[6144,128]{1,0:T(8,128)(2,1)S(1)} %shard_map.67.chosen_ref, f32[2,3,768]{2,1,0:T(4,128)S(1)} %get-tuple-element.48.rest_6_.rest_0_, f32[1,3,768]{2,1,0:T(4,128)S(1)} %get-tuple-element.49.rest_10_.rest_1_, ...), custom_call_target="tpu_custom_call" | custom-call | tf_op jit(solution)/shard_map/pallas_call | solution.py:536
  (19 shorter events, 0.1 us)
Async XLA Ops:
  0.0 0.7 %copy-start.6 = (bf16[1,24,128]{2,1,0:T(8,128)(2,1)S(1)}, bf16[1,24,128]{2,1,0:T(8,128)(2,1)}, u32[]{:S(2)}) copy-start(bf16[1,24,128]{2,1,0:T(8,128)(2,1)} %param.6) | copy-start | bytes 18436
  0.0 29.0 %copy-start.1 = (bf16[6,1030,128]{2,1,0:T(8,128)(2,1)S(1)}, bf16[6,1030,128]{2,1,0:T(8,128)(2,1)}, u32[]{:S(2)}) copy-start(bf16[6,1030,128]{2,1,0:T(8,128)(2,1)} %all_pages_ref.1) | copy-start | bytes 4746244
  0.0 29.0 %copy-start = (s32[256]{0:T(256)S(1)}, s32[256]{0:T(256)}, u32[]{:S(2)}) copy-start(s32[256]{0:T(256)} %len_hbm.1) | copy-start | bytes 3076
  0.0 29.0 %copy-start.4 = (s32[6]{0:T(128)S(1)}, s32[6]{0:T(128)}, u32[]{:S(2)}) copy-start(s32[6]{0:T(128)} %helper_hbm.1) | copy-start | bytes 76
  0.0 29.0 %copy-start.3 = (s32[3]{0:T(128)S(1)}, s32[3]{0:T(128)}, u32[]{:S(2)}) copy-start(s32[3]{0:T(128)} %offset_hbm.1) | copy-start | bytes 40
  0.0 29.0 %copy-start.2 = (s32[3]{0:T(128)S(1)}, s32[3]{0:T(128)}, u32[]{:S(2)}) copy-start(s32[3]{0:T(128)} %count_hbm.1) | copy-start | bytes 40
  22.0 7.1 %collective-permute-start.1 = (bf16[32,24,128]{2,1,0:T(8,128)(2,1)S(1)}, bf16[32,24,128]{2,1,0:T(8,128)(2,1)S(1)}, u32[]{:S(2)}, u32[]{:S(2)}) collective-permute-start(bf16[32,24,128]{2,1,0:T(8,128)(2,1)S(1)} %all_to_all.5.rest_0_), channel_id=1, source_target_pairs={{0,1},{1,0},{2,3},{3,2},{4,5},{5,4},{6,7},{7,6},{8,9},{9,8},{10,11... | collective-permute-start | bytes 589832 | tf_op jit(solution)/shard_map/ppermute | solution.py:42
  24.8 9.6 %collective-permute-start = (bf16[32,24,128]{2,1,0:T(8,128)(2,1)S(1)}, bf16[32,24,128]{2,1,0:T(8,128)(2,1)S(1)}, u32[]{:S(2)}, u32[]{:S(2)}) collective-permute-start(bf16[32,24,128]{2,1,0:T(8,128)(2,1)S(1)} %all_to_all.5.rest_0_), channel_id=1, source_target_pairs={{0,128},{1,129},{2,130},{3,131},{4,132},{5,133},{6,134},{7,135},{8... | collective-permute-start | bytes 589832 | tf_op jit(solution)/shard_map/ppermute | solution.py:37
  27.6 9.6 %collective-permute-start.3 = (bf16[32,24,128]{2,1,0:T(8,128)(2,1)S(1)}, bf16[32,24,128]{2,1,0:T(8,128)(2,1)S(1)}, u32[]{:S(2)}, u32[]{:S(2)}) collective-permute-start(bf16[32,24,128]{2,1,0:T(8,128)(2,1)S(1)} %all_to_all.5.rest_0_), channel_id=1, source_target_pairs={{0,144},{1,145},{2,146},{3,147},{4,148},{5,149},{6,150},{7,151},{8... | collective-permute-start | bytes 589832 | tf_op jit(solution)/shard_map/ppermute | solution.py:37
  28.4 8.8 %collective-permute-start.2 = (bf16[32,24,128]{2,1,0:T(8,128)(2,1)S(1)}, bf16[32,24,128]{2,1,0:T(8,128)(2,1)S(1)}, u32[]{:S(2)}, u32[]{:S(2)}) collective-permute-start(bf16[32,24,128]{2,1,0:T(8,128)(2,1)S(1)} %all_to_all.5.rest_0_), channel_id=1, source_target_pairs={{0,16},{1,17},{2,18},{3,19},{4,20},{5,21},{6,22},{7,23},{8,24},{9,... | collective-permute-start | bytes 589832 | tf_op jit(solution)/shard_map/ppermute | solution.py:37
  37.2 2.5 %collective-permute-start.4 = (bf16[32,24,128]{2,1,0:T(8,128)(2,1)S(1)}, bf16[32,24,128]{2,1,0:T(8,128)(2,1)S(1)}, u32[]{:S(2)}, u32[]{:S(2)}) collective-permute-start(bf16[32,24,128]{2,1,0:T(8,128)(2,1)S(1)} %collective-permute-done.rest_0_), channel_id=1, source_target_pairs={{0,1},{1,0},{2,3},{3,2},{4,5},{5,4},{6,7},{7,6},{8,9},{9,8},{10,11... | collective-permute-start | bytes 589832 | tf_op jit(solution)/shard_map/ppermute | solution.py:42
  38.0 1.7 %collective-permute-start.5 = (bf16[32,24,128]{2,1,0:T(8,128)(2,1)S(1)}, bf16[32,24,128]{2,1,0:T(8,128)(2,1)S(1)}, u32[]{:S(2)}, u32[]{:S(2)}) collective-permute-start(bf16[32,24,128]{2,1,0:T(8,128)(2,1)S(1)} %collective-permute-done.2.rest_1_), channel_id=1, source_target_pairs={{0,1},{1,0},{2,3},{3,2},{4,5},{5,4},{6,7},{7,6},{8,9},{9,8},{10,11... | collective-permute-start | bytes 589832 | tf_op jit(solution)/shard_map/ppermute | solution.py:42
  38.0 1.7 %collective-permute-start.6 = (bf16[32,24,128]{2,1,0:T(8,128)(2,1)S(1)}, bf16[32,24,128]{2,1,0:T(8,128)(2,1)S(1)}, u32[]{:S(2)}, u32[]{:S(2)}) collective-permute-start(bf16[32,24,128]{2,1,0:T(8,128)(2,1)S(1)} %collective-permute-done.3.rest_3_), channel_id=1, source_target_pairs={{0,1},{1,0},{2,3},{3,2},{4,5},{5,4},{6,7},{7,6},{8,9},{9,8},{10,11... | collective-permute-start | bytes 589832 | tf_op jit(solution)/shard_map/ppermute | solution.py:42
  38.5 1.2 %copy-start.5 = (f32[8,128]{1,0:T(8,128)S(1)}, f32[8,128]{1,0:T(8,128)}, u32[]{:S(2)}) copy-start(f32[8,128]{1,0:T(8,128)} %shard_map.64.nothing_ref) | copy-start | bytes 12292
  45.3 7.8 %collective-permute-start.7 = (f32[3,6144]{1,0:T(4,128)S(1)}, f32[3,6144]{1,0:T(4,128)S(1)}, u32[]{:S(2)}, u32[]{:S(2)}) collective-permute-start(f32[3,6144]{1,0:T(4,128)S(1)} %get-tuple-element.64), channel_id=1, source_target_pairs={{0,29},{1,30},{2,31},{3,0},{4,1},{5,2},{6,3},{7,4},{8,5},{9,6},{10... | collective-permute-start | bytes 221192 | tf_op jit(solution)/shard_map/ppermute | solution.py:50
  45.4 7.7 %collective-permute-start.8 = (f32[3,6144]{1,0:T(4,128)S(1)}, f32[3,6144]{1,0:T(4,128)S(1)}, u32[]{:S(2)}, u32[]{:S(2)}) collective-permute-start(f32[3,6144]{1,0:T(4,128)S(1)} %get-tuple-element.65), channel_id=1, source_target_pairs={{0,31},{1,0},{2,1},{3,2},{4,3},{5,4},{6,5},{7,6},{8,7},{9,8},{10,9... | collective-permute-start | bytes 221192 | tf_op jit(solution)/shard_map/ppermute | solution.py:50
  48.0 5.3 %collective-permute-start.9 = (f32[3,6144]{1,0:T(4,128)S(1)}, f32[3,6144]{1,0:T(4,128)S(1)}, u32[]{:S(2)}, u32[]{:S(2)}) collective-permute-start(f32[3,6144]{1,0:T(4,128)S(1)} %get-tuple-element.66), channel_id=1, source_target_pairs={{0,30},{1,31},{2,0},{3,1},{4,2},{5,3},{6,4},{7,5},{8,6},{9,7},{10,... | collective-permute-start | bytes 221192 | tf_op jit(solution)/shard_map/ppermute | solution.py:50

commit v6 on v5

--- a/solution.py
+++ b/solution.py
@@ -496,7 +496,7 @@
     )(plan, two, pages)
 
     one, two, three, far_out = lax.optimization_barrier((one, two, three, far_out))
-    two_other, one_other, three_other = [other_core(value) for value in (two, one, three)]
+    three_other, one_other, two_other = [other_core(value) for value in (three, one, two)]
     chosen = pl.pallas_call(
         chosen_kernel,
         out_shape=jax.ShapeDtypeStruct((columns, total // 2), jnp.bfloat16),

time: 54.7 us -> 54.6 us (level)
  Pallas kernels: 21.8 us -> 20.6 us
  starting transfers between devices: 11 us -> 11.6 us
  waiting for transfers between devices: 0.46 us -> 1.01 us
    ppermute x3, starting transfers between devices: 2.67 us -> 3.27 us  [along_blk(): return lax.ppermute(value, AXES, pairs)]
    pallas_call x1, Pallas kernels: 5.58 us -> 4.98 us  [local(): pl.pallas_call(functools.partial(late_kernel, rest, (own, far), total), o...]
    pallas_call x1, Pallas kernels: 5.13 us -> 4.53 us  [local(): pl.pallas_call(functools.partial(home_kernel, rest, total), out_shape=par...]
    ppermute x3, waiting for transfers between devices: 0.15 us -> 0.7 us  [along_blk(): return lax.ppermute(value, AXES, pairs)]
  transfers between devices with their start and end apart: 10 -> 10, of which waited for: 2 -> 3; matrix products, arithmetic and copies ran while one was open for 0% -> 0% of each run, Pallas kernels for 26% -> 25%
where the time goes in v6:
time: 54.6 us; the launch traced here: 54.7 us
  blocking collectives  21.2 us (39%)
  Pallas kernels  20.6 us (38%)
  starting transfers between devices  11.6 us (21%)
  waiting for transfers between devices  1.01 us (2%)
    all_to_all x1, blocking collectives, local(): mine = lax.all_to_all(copies, ('y', 'z'), 0, 0, tiled=True)  21.2 us
    pallas_call x1, Pallas kernels, local(): pl.pallas_call(functools.partial(first_kernel, own), out_shape=part(own)...  5.32 us
    pallas_call x1, Pallas kernels, local(): pl.pallas_call(functools.partial(late_kernel, rest, (own, far), total), o...  4.98 us
    pallas_call x1, Pallas kernels, local(): pl.pallas_call(functools.partial(home_kernel, rest, total), out_shape=par...  4.53 us
    ppermute x3, starting transfers between devices, along_x(): return lax.ppermute(value, AXES, pairs)  4.21 us
    ppermute x4, starting transfers between devices, other_core(): return lax.ppermute(value, AXES, pairs)  4.14 us
    ppermute x3, starting transfers between devices, along_blk(): return lax.ppermute(value, AXES, pairs)  3.27 us
    pallas_call x1, Pallas kernels, local(): pl.pallas_call(functools.partial(more_kernel, far, total), out_shape=part...  2.5 us
  transfers between devices with their start and end apart: 10, of which 3 were waited for; matrix products, arithmetic and copies ran while one was open for 0% of the time, Pallas kernels for 25%

profile of v6, /device:TPU:1, one launch (start us, length us, event | category | flops | bytes accessed | tf_op | source)
XLA Modules:
  0.0 54.7 jit_solution(14038989971769277754)
XLA Ops:
  0.0 0.6 %shard_map.64.nothing_ref = f32[8,128]{1,0:T(8,128)} custom-call(), custom_call_target="tpu_custom_call" | custom-call | flops 9720299520 | bytes 1582080 | tf_op jit(solution)/shard_map/pallas_call | solution.py:455
  0.6 0.1 copy-done.6
  0.7 21.2 %all_to_all.5.rest_0_ = bf16[32,24,128]{2,1,0:T(8,128)(2,1)S(1)} all-to-all(bf16[32,24,128]{2,1,0:T(8,128)(2,1)S(1)} %broadcast_in_dim.11), channel_id=1, replica_groups=mesh['xh'=2,'y'=4,'xl'=2,'z'=8,'c'=2] {'y','z'}, dimensions={0} | all-to-all | bytes 393216 | tf_op jit(solution)/shard_map/all_to_all | solution.py:463
  22.0 2.8 %collective-permute-start.1 = (bf16[32,24,128]{2,1,0:T(8,128)(2,1)S(1)}, bf16[32,24,128]{2,1,0:T(8,128)(2,1)S(1)}, u32[]{:S(2)}, u32[]{:S(2)}) collective-permute-start(bf16[32,24,128]{2,1,0:T(8,128)(2,1)S(1)} %all_to_all.5.rest_0_), channel_id=1, source_target_pairs={{0,1},{1,0},{2,3},{3,2},{4,5},{5,4},{6,7},{7,6},{8,9},{9,8},{10,11... | collective-permute-start | bytes 589832 | tf_op jit(solution)/shard_map/ppermute | solution.py:42
  24.8 2.7 %collective-permute-start = (bf16[32,24,128]{2,1,0:T(8,128)(2,1)S(1)}, bf16[32,24,128]{2,1,0:T(8,128)(2,1)S(1)}, u32[]{:S(2)}, u32[]{:S(2)}) collective-permute-start(bf16[32,24,128]{2,1,0:T(8,128)(2,1)S(1)} %all_to_all.5.rest_0_), channel_id=1, source_target_pairs={{0,128},{1,129},{2,130},{3,131},{4,132},{5,133},{6,134},{7,135},{8... | collective-permute-start | bytes 589832 | tf_op jit(solution)/shard_map/ppermute | solution.py:37
  27.6 0.9 %collective-permute-start.3 = (bf16[32,24,128]{2,1,0:T(8,128)(2,1)S(1)}, bf16[32,24,128]{2,1,0:T(8,128)(2,1)S(1)}, u32[]{:S(2)}, u32[]{:S(2)}) collective-permute-start(bf16[32,24,128]{2,1,0:T(8,128)(2,1)S(1)} %all_to_all.5.rest_0_), channel_id=1, source_target_pairs={{0,144},{1,145},{2,146},{3,147},{4,148},{5,149},{6,150},{7,151},{8... | collective-permute-start | bytes 589832 | tf_op jit(solution)/shard_map/ppermute | solution.py:37
  28.4 0.6 %collective-permute-start.2 = (bf16[32,24,128]{2,1,0:T(8,128)(2,1)S(1)}, bf16[32,24,128]{2,1,0:T(8,128)(2,1)S(1)}, u32[]{:S(2)}, u32[]{:S(2)}) collective-permute-start(bf16[32,24,128]{2,1,0:T(8,128)(2,1)S(1)} %all_to_all.5.rest_0_), channel_id=1, source_target_pairs={{0,16},{1,17},{2,18},{3,19},{4,20},{5,21},{6,22},{7,23},{8,24},{9,... | collective-permute-start | bytes 589832 | tf_op jit(solution)/shard_map/ppermute | solution.py:37
  29.1 5.3 %shard_map.65 = (f32[2,3,768]{2,1,0:T(4,128)S(1)}, f32[2,3,768]{2,1,0:T(4,128)S(1)}, f32[2,3,768]{2,1,0:T(4,128)S(1)}, f32[2,3,768]{2,1,0:T(4,128)S(1)}, s32[270]{0:T(512)S(1)}) custom-call(s32[256]{0:T(256)S(1)} %copy-done, s32[3]{0:T(128)S(1)} %copy-done.2, s32[3]{0:T(128)S(1)} %copy-done.3, s32[6]{0:T(128)S(1)} %copy-done.4, ...), custom_call_target="tpu_custom_call" | custom-call | flops 1101004800 | bytes 179200 | tf_op jit(solution)/shard_map/pallas_call | solution.py:467
  34.4 0.0 collective-permute-done.rest_0_
  34.4 2.5 %shard_map.66 = (f32[1,3,768]{2,1,0:T(4,128)S(1)}, f32[1,3,768]{2,1,0:T(4,128)S(1)}, f32[1,3,768]{2,1,0:T(4,128)S(1)}, f32[1,3,768]{2,1,0:T(4,128)S(1)}) custom-call(s32[270]{0:T(512)S(1)} %get-tuple-element.38.plan_ref, bf16[32,24,128]{2,1,0:T(8,128)(2,1)S(1)} %collective-permute-done.rest_0_, bf16[6,1030,128]{2,1,0:T(8,128)(2,1)S(1)} %copy-done.1), custom_call_target="tpu_custom_call" | custom-call | flops 1101004800 | bytes 179200 | tf_op jit(solution)/shard_map/pallas_call | solution.py:488
  36.9 0.3 collective-permute-done.3.rest_3_
  37.2 0.8 %collective-permute-start.4 = (bf16[32,24,128]{2,1,0:T(8,128)(2,1)S(1)}, bf16[32,24,128]{2,1,0:T(8,128)(2,1)S(1)}, u32[]{:S(2)}, u32[]{:S(2)}) collective-permute-start(bf16[32,24,128]{2,1,0:T(8,128)(2,1)S(1)} %collective-permute-done.rest_0_), channel_id=1, source_target_pairs={{0,1},{1,0},{2,3},{3,2},{4,5},{5,4},{6,7},{7,6},{8,9},{9,8},{10,11... | collective-permute-start | bytes 589832 | tf_op jit(solution)/shard_map/ppermute | solution.py:42
  38.0 0.0 collective-permute-start.5
  38.0 0.5 collective-permute-start.6
  38.5 1.2 %shard_map.67.chosen_ref = bf16[6144,128]{1,0:T(8,128)(2,1)S(1)} custom-call(s32[270]{0:T(512)S(1)} %get-tuple-element.38.plan_ref, s32[1,256]{1,0:T(1,128)S(1)} %bitcast.2), custom_call_target="tpu_custom_call" | custom-call | flops 1620049920 | bytes 263680 | tf_op jit(solution)/shard_map/pallas_call | solution.py:500
  39.7 0.0 collective-permute-done.4.rest_0_
  39.7 0.0 collective-permute-done.6.rest_4_
  39.7 5.0 %shard_map.68 = (f32[3,6144]{1,0:T(4,128)S(1)}, f32[3,6144]{1,0:T(4,128)S(1)}, f32[3,6144]{1,0:T(4,128)S(1)}, f32[3,6144]{1,0:T(4,128)S(1)}, bf16[4864,128]{1,0:T(8,128)(2,1)S(1)}) custom-call(s32[270]{0:T(512)S(1)} %get-tuple-element.38.plan_ref, f32[8,128]{1,0:T(8,128)S(1)} %copy-done.5, bf16[32,24,128]{2,1,0:T(8,128)(2,1)S(1)} %collective-permute-done.4.rest_0_, ...), custom_call_target="tpu_custom_call" | custom-call | flops 4860149760 | bytes 791040 | tf_op jit(solution)/shard_map/pallas_call | solution.py:511
  44.7 0.7 %collective-permute-start.7 = (f32[3,6144]{1,0:T(4,128)S(1)}, f32[3,6144]{1,0:T(4,128)S(1)}, u32[]{:S(2)}, u32[]{:S(2)}) collective-permute-start(f32[3,6144]{1,0:T(4,128)S(1)} %get-tuple-element.64), channel_id=1, source_target_pairs={{0,29},{1,30},{2,31},{3,0},{4,1},{5,2},{6,3},{7,4},{8,5},{9,6},{10... | collective-permute-start | bytes 221192 | tf_op jit(solution)/shard_map/ppermute | solution.py:50
  45.4 2.5 %collective-permute-start.8 = (f32[3,6144]{1,0:T(4,128)S(1)}, f32[3,6144]{1,0:T(4,128)S(1)}, u32[]{:S(2)}, u32[]{:S(2)}) collective-permute-start(f32[3,6144]{1,0:T(4,128)S(1)} %get-tuple-element.65), channel_id=1, source_target_pairs={{0,31},{1,0},{2,1},{3,2},{4,3},{5,4},{6,5},{7,6},{8,7},{9,8},{10,9... | collective-permute-start | bytes 221192 | tf_op jit(solution)/shard_map/ppermute | solution.py:50
  48.0 4.5 %shard_map.69.rest_2_ = f32[5,3,768]{2,1,0:T(4,128)S(1)} custom-call(s32[270]{0:T(512)S(1)} %get-tuple-element.38.plan_ref, bf16[4864,128]{1,0:T(8,128)(2,1)S(1)} %get-tuple-element.62.kept_ref, bf16[6,1030,128]{2,1,0:T(8,128)(2,1)S(1)} %copy-done.1, f32[3,6144]{1,0:T(4,128)S(1)} %get-tuple-element.63.before_ref), custom_call_target="tpu_custom_call" | custom-call | flops 4860149760 | bytes 791040 | tf_op jit(solution)/shard_map/pallas_call | solution.py:526
  52.5 0.2 collective-permute-done.8.rest_4_
  52.7 0.5 collective-permute-done.9.rest_5_
  53.2 1.5 %shard_map.70 = f32[3,256]{1,0:T(4,128)} custom-call(s32[270]{0:T(512)S(1)} %get-tuple-element.38.plan_ref, s32[1,256]{1,0:T(1,128)S(1)} %bitcast.3, bf16[6144,128]{1,0:T(8,128)(2,1)S(1)} %shard_map.67.chosen_ref, f32[2,3,768]{2,1,0:T(4,128)S(1)} %get-tuple-element.48.rest_6_.rest_0_, f32[1,3,768]{2,1,0:T(4,128)S(1)} %get-tuple-element.49.rest_10_.rest_1_, ...), custom_call_target="tpu_custom_call" | custom-call | tf_op jit(solution)/shard_map/pallas_call | solution.py:536
  (19 shorter events, 0.1 us)
Async XLA Ops:
  0.0 0.7 %copy-start.6 = (bf16[1,24,128]{2,1,0:T(8,128)(2,1)S(1)}, bf16[1,24,128]{2,1,0:T(8,128)(2,1)}, u32[]{:S(2)}) copy-start(bf16[1,24,128]{2,1,0:T(8,128)(2,1)} %param.6) | copy-start | bytes 18436
  0.0 29.0 %copy-start.1 = (bf16[6,1030,128]{2,1,0:T(8,128)(2,1)S(1)}, bf16[6,1030,128]{2,1,0:T(8,128)(2,1)}, u32[]{:S(2)}) copy-start(bf16[6,1030,128]{2,1,0:T(8,128)(2,1)} %all_pages_ref.1) | copy-start | bytes 4746244
  0.0 29.0 %copy-start = (s32[256]{0:T(256)S(1)}, s32[256]{0:T(256)}, u32[]{:S(2)}) copy-start(s32[256]{0:T(256)} %len_hbm.1) | copy-start | bytes 3076
  0.0 29.0 %copy-start.4 = (s32[6]{0:T(128)S(1)}, s32[6]{0:T(128)}, u32[]{:S(2)}) copy-start(s32[6]{0:T(128)} %helper_hbm.1) | copy-start | bytes 76
  0.0 29.0 %copy-start.3 = (s32[3]{0:T(128)S(1)}, s32[3]{0:T(128)}, u32[]{:S(2)}) copy-start(s32[3]{0:T(128)} %offset_hbm.1) | copy-start | bytes 40
  0.0 29.0 %copy-start.2 = (s32[3]{0:T(128)S(1)}, s32[3]{0:T(128)}, u32[]{:S(2)}) copy-start(s32[3]{0:T(128)} %count_hbm.1) | copy-start | bytes 40
  22.0 7.1 %collective-permute-start.1 = (bf16[32,24,128]{2,1,0:T(8,128)(2,1)S(1)}, bf16[32,24,128]{2,1,0:T(8,128)(2,1)S(1)}, u32[]{:S(2)}, u32[]{:S(2)}) collective-permute-start(bf16[32,24,128]{2,1,0:T(8,128)(2,1)S(1)} %all_to_all.5.rest_0_), channel_id=1, source_target_pairs={{0,1},{1,0},{2,3},{3,2},{4,5},{5,4},{6,7},{7,6},{8,9},{9,8},{10,11... | collective-permute-start | bytes 589832 | tf_op jit(solution)/shard_map/ppermute | solution.py:42
  24.8 9.6 %collective-permute-start = (bf16[32,24,128]{2,1,0:T(8,128)(2,1)S(1)}, bf16[32,24,128]{2,1,0:T(8,128)(2,1)S(1)}, u32[]{:S(2)}, u32[]{:S(2)}) collective-permute-start(bf16[32,24,128]{2,1,0:T(8,128)(2,1)S(1)} %all_to_all.5.rest_0_), channel_id=1, source_target_pairs={{0,128},{1,129},{2,130},{3,131},{4,132},{5,133},{6,134},{7,135},{8... | collective-permute-start | bytes 589832 | tf_op jit(solution)/shard_map/ppermute | solution.py:37
  27.6 9.6 %collective-permute-start.3 = (bf16[32,24,128]{2,1,0:T(8,128)(2,1)S(1)}, bf16[32,24,128]{2,1,0:T(8,128)(2,1)S(1)}, u32[]{:S(2)}, u32[]{:S(2)}) collective-permute-start(bf16[32,24,128]{2,1,0:T(8,128)(2,1)S(1)} %all_to_all.5.rest_0_), channel_id=1, source_target_pairs={{0,144},{1,145},{2,146},{3,147},{4,148},{5,149},{6,150},{7,151},{8... | collective-permute-start | bytes 589832 | tf_op jit(solution)/shard_map/ppermute | solution.py:37
  28.4 8.8 %collective-permute-start.2 = (bf16[32,24,128]{2,1,0:T(8,128)(2,1)S(1)}, bf16[32,24,128]{2,1,0:T(8,128)(2,1)S(1)}, u32[]{:S(2)}, u32[]{:S(2)}) collective-permute-start(bf16[32,24,128]{2,1,0:T(8,128)(2,1)S(1)} %all_to_all.5.rest_0_), channel_id=1, source_target_pairs={{0,16},{1,17},{2,18},{3,19},{4,20},{5,21},{6,22},{7,23},{8,24},{9,... | collective-permute-start | bytes 589832 | tf_op jit(solution)/shard_map/ppermute | solution.py:37
  37.2 2.5 %collective-permute-start.4 = (bf16[32,24,128]{2,1,0:T(8,128)(2,1)S(1)}, bf16[32,24,128]{2,1,0:T(8,128)(2,1)S(1)}, u32[]{:S(2)}, u32[]{:S(2)}) collective-permute-start(bf16[32,24,128]{2,1,0:T(8,128)(2,1)S(1)} %collective-permute-done.rest_0_), channel_id=1, source_target_pairs={{0,1},{1,0},{2,3},{3,2},{4,5},{5,4},{6,7},{7,6},{8,9},{9,8},{10,11... | collective-permute-start | bytes 589832 | tf_op jit(solution)/shard_map/ppermute | solution.py:42
  38.0 1.7 %collective-permute-start.5 = (bf16[32,24,128]{2,1,0:T(8,128)(2,1)S(1)}, bf16[32,24,128]{2,1,0:T(8,128)(2,1)S(1)}, u32[]{:S(2)}, u32[]{:S(2)}) collective-permute-start(bf16[32,24,128]{2,1,0:T(8,128)(2,1)S(1)} %collective-permute-done.2.rest_1_), channel_id=1, source_target_pairs={{0,1},{1,0},{2,3},{3,2},{4,5},{5,4},{6,7},{7,6},{8,9},{9,8},{10,11... | collective-permute-start | bytes 589832 | tf_op jit(solution)/shard_map/ppermute | solution.py:42
  38.0 1.7 %collective-permute-start.6 = (bf16[32,24,128]{2,1,0:T(8,128)(2,1)S(1)}, bf16[32,24,128]{2,1,0:T(8,128)(2,1)S(1)}, u32[]{:S(2)}, u32[]{:S(2)}) collective-permute-start(bf16[32,24,128]{2,1,0:T(8,128)(2,1)S(1)} %collective-permute-done.3.rest_3_), channel_id=1, source_target_pairs={{0,1},{1,0},{2,3},{3,2},{4,5},{5,4},{6,7},{7,6},{8,9},{9,8},{10,11... | collective-permute-start | bytes 589832 | tf_op jit(solution)/shard_map/ppermute | solution.py:42
  38.5 1.2 %copy-start.5 = (f32[8,128]{1,0:T(8,128)S(1)}, f32[8,128]{1,0:T(8,128)}, u32[]{:S(2)}) copy-start(f32[8,128]{1,0:T(8,128)} %shard_map.64.nothing_ref) | copy-start | bytes 12292
  44.7 7.8 %collective-permute-start.7 = (f32[3,6144]{1,0:T(4,128)S(1)}, f32[3,6144]{1,0:T(4,128)S(1)}, u32[]{:S(2)}, u32[]{:S(2)}) collective-permute-start(f32[3,6144]{1,0:T(4,128)S(1)} %get-tuple-element.64), channel_id=1, source_target_pairs={{0,29},{1,30},{2,31},{3,0},{4,1},{5,2},{6,3},{7,4},{8,5},{9,6},{10... | collective-permute-start | bytes 221192 | tf_op jit(solution)/shard_map/ppermute | solution.py:50
  45.4 7.2 %collective-permute-start.8 = (f32[3,6144]{1,0:T(4,128)S(1)}, f32[3,6144]{1,0:T(4,128)S(1)}, u32[]{:S(2)}, u32[]{:S(2)}) collective-permute-start(f32[3,6144]{1,0:T(4,128)S(1)} %get-tuple-element.65), channel_id=1, source_target_pairs={{0,31},{1,0},{2,1},{3,2},{4,3},{5,4},{6,5},{7,6},{8,7},{9,8},{10,9... | collective-permute-start | bytes 221192 | tf_op jit(solution)/shard_map/ppermute | solution.py:50
  48.0 5.2 %collective-permute-start.9 = (f32[3,6144]{1,0:T(4,128)S(1)}, f32[3,6144]{1,0:T(4,128)S(1)}, u32[]{:S(2)}, u32[]{:S(2)}) collective-permute-start(f32[3,6144]{1,0:T(4,128)S(1)} %get-tuple-element.66), channel_id=1, source_target_pairs={{0,30},{1,31},{2,0},{3,1},{4,2},{5,3},{6,4},{7,5},{8,6},{9,7},{10,... | collective-permute-start | bytes 221192 | tf_op jit(solution)/shard_map/ppermute | solution.py:50
